TPU v7x, 128 devices: a whole 4x4x4 slice. The times are simulated.
128 devices in a mesh: seq: 16 (over z, y), tp: 8 (over x, core).
Axes of the slice: x: 4, y: 4, z: 4, core: 2. Of those that a mesh axis runs over, the one named last changes fastest.
Arguments:
- tokens: bfloat16 [8192, 4096], P('seq'), may hold values from -6 to 6
- norm_gain: float32 [4096], replicated, may hold values from 0.1 to 1.9
- w_query: bfloat16 [4096, 4096], P(None, 'tp'), may hold values from -2.5 to 2.5
- w_key: bfloat16 [4096, 1024], P(None, 'tp'), may hold values from -0.09375 to 0.09375
- w_value: bfloat16 [4096, 1024], P(None, 'tp'), may hold values from -0.09375 to 0.09375
- w_out: bfloat16 [4096, 4096], P('tp'), may hold values from -0.75 to 0.75
- doc_ids: int32 [64], replicated, may hold values from 0 to 7, never falling along the last dimension, each value on 1 to 36 neighbouring positions
Outputs:
- attended: bfloat16 [8192, 4096], P(('seq', 'tp'))
Inputs may be any that keep to these rules, and one draw needn't show every extreme that they name: `doc_ids`: never decreasing; each document covers 1 to 36 blocks and one covers exactly 36.
All inputs are finite; a program needn't handle non-finite values.
Results may differ from a plain program's by a relative error of at most 0.019.
Values may be sent and summed in bfloat16 or wider, within the bound.
A program may use at most 64 MiB of HBM per device.

v0:
```python
import math

import jax
import jax.numpy as jnp
from jax import lax
from jax.sharding import PartitionSpec as P

HD = 128
BLK = 128


floor_score = -1e30
rope_base = 500000.0
norm_epsilon = 1e-05


def document_starts(doc_ids):
    earlier = doc_ids[None, :] < doc_ids[:, None]
    return jnp.sum(earlier.astype(jnp.int32), axis=1) * BLK


def token_starts(positions, block_starts):
    blocks = positions // BLK
    block_count = block_starts.shape[0]
    matches = blocks[..., None] == jnp.arange(block_count, dtype=jnp.int32)
    return jnp.sum(jnp.where(matches, block_starts, 0), axis=-1)


def rotate(values, offsets):
    half_dim = HD // 2
    inverse = jnp.exp(jnp.arange(half_dim, dtype=jnp.float32) * (-2.0 * math.log(rope_base) / HD))
    angles = offsets.astype(jnp.float32)[:, None] * inverse[None, :]
    cos_term = jnp.cos(angles)[:, None, :]
    sin_term = jnp.sin(angles)[:, None, :]
    first_half = values[..., :half_dim]
    second_half = values[..., half_dim:]
    return jnp.concatenate(
        [
            first_half * cos_term - second_half * sin_term,
            second_half * cos_term + first_half * sin_term,
        ],
        axis=-1,
    )


def normalize(tokens, norm_gain):
    floats = tokens.astype(jnp.float32)
    squares = jnp.mean(floats * floats, axis=-1, keepdims=True)
    return (floats * lax.rsqrt(squares + norm_epsilon) * norm_gain).astype(jnp.bfloat16)


def gathered_keys(fold_keys, initial, kv_pairs):
    return fold_keys(initial, lax.all_gather(kv_pairs, "seq", axis=0, tiled=True), jnp.int32(0))


def attend(queries, positions, block_starts, kv_heads, collect):
    total_rows = queries.shape[0]
    groups = total_rows // BLK
    q_heads = queries.shape[1] // HD
    per_group = q_heads // kv_heads
    kv_cols = kv_heads * HD
    starts = token_starts(positions, block_starts)
    tok_pos = positions.reshape(groups, BLK)
    tok_start = starts.reshape(groups, BLK)
    row_pos = jnp.repeat(tok_pos, per_group, axis=1)
    row_start = jnp.repeat(tok_start, per_group, axis=1)
    grouped = (
        queries.reshape(groups, BLK, kv_heads, per_group, HD)
        .transpose(0, 2, 1, 3, 4)
        .reshape(groups, kv_heads, BLK * per_group, HD)
    )
    score_scale = HD ** (-0.5)
    width_rows = BLK * per_group
    initial = (
        jnp.full((groups, kv_heads, width_rows), floor_score, jnp.float32),
        jnp.zeros((groups, kv_heads, width_rows), jnp.float32),
        jnp.zeros((groups, kv_heads, width_rows, HD), jnp.float32),
    )

    def update(running, group_index, key_block, value_block, key_pos):
        maxima, totals, weighted = running
        query_block = lax.dynamic_index_in_dim(grouped, group_index, 0, keepdims=False)
        rows_pos = lax.dynamic_index_in_dim(row_pos, group_index, 0, keepdims=False)
        rows_start = lax.dynamic_index_in_dim(row_start, group_index, 0, keepdims=False)
        scores = (
            jnp.einsum("hrd,khd->hrk", query_block, key_block, preferred_element_type=jnp.float32)
            * score_scale
        )
        allowed = (key_pos[None, :] >= rows_start[:, None]) & (
            key_pos[None, :] <= rows_pos[:, None]
        )
        scores = jnp.where(allowed[None], scores, floor_score)
        old_max = maxima[group_index]
        new_max = jnp.maximum(old_max, jnp.max(scores, axis=-1))
        factor = jnp.exp(old_max - new_max)
        weights = jnp.where(allowed[None], jnp.exp(scores - new_max[..., None]), 0.0)
        new_total = factor * totals[group_index] + jnp.sum(weights, axis=-1)
        new_sum = factor[..., None] * weighted[group_index] + jnp.einsum(
            "hrk,khd->hrd",
            weights.astype(jnp.bfloat16),
            value_block,
            preferred_element_type=jnp.float32,
        )
        return (
            maxima.at[group_index].set(new_max),
            totals.at[group_index].set(new_total),
            weighted.at[group_index].set(new_sum),
        )

    def fold_keys(running, kv_piece, first_row):
        length = kv_piece.shape[0]
        key_width = math.gcd(length, BLK)
        key_steps = length // key_width
        key_split = kv_piece[:, :kv_cols].reshape(key_steps, key_width, kv_heads, HD)
        value_split = kv_piece[:, kv_cols:].reshape(key_steps, key_width, kv_heads, HD)

        def over_keys(key_step, running):
            key_block = lax.dynamic_index_in_dim(key_split, key_step, 0, keepdims=False)
            value_block = lax.dynamic_index_in_dim(value_split, key_step, 0, keepdims=False)
            block_first = key_step * key_width
            key_pos = block_first + jnp.arange(key_width, dtype=jnp.int32)

            def over_groups(group_index, running):
                needed = jnp.any(
                    (block_first + key_width > tok_start[group_index])
                    & (block_first <= tok_pos[group_index])
                )
                return lax.cond(
                    needed,
                    lambda current: update(current, group_index, key_block, value_block, key_pos),
                    lambda current: current,
                    running,
                )

            return lax.fori_loop(0, groups, over_groups, running)

        return lax.fori_loop(0, key_steps, over_keys, running)

    maxima, totals, weighted = collect(fold_keys, initial)
    context = (weighted / totals[..., None]).astype(jnp.bfloat16)
    return (
        context.reshape(groups, kv_heads, BLK, per_group, HD)
        .transpose(0, 2, 1, 3, 4)
        .reshape(total_rows, q_heads * HD)
    )


def local(tokens, norm_gain, w_query, w_key, w_value, w_out, doc_ids):
    local_rows = tokens.shape[0]
    seq_index = lax.axis_index("seq")
    normed = normalize(tokens, norm_gain)
    q_heads = w_query.shape[1] // HD
    kv_heads = w_key.shape[1] // HD
    query_raw = jnp.dot(normed, w_query, preferred_element_type=jnp.float32)
    key_raw = jnp.dot(normed, w_key, preferred_element_type=jnp.float32)
    values = jnp.dot(normed, w_value, preferred_element_type=jnp.float32).astype(jnp.bfloat16)
    block_starts = document_starts(doc_ids)
    positions = seq_index * local_rows + jnp.arange(local_rows, dtype=jnp.int32)
    offsets = positions - token_starts(positions, block_starts)
    queries = (
        rotate(query_raw.reshape(local_rows, q_heads, HD), offsets)
        .astype(jnp.bfloat16)
        .reshape(local_rows, q_heads * HD)
    )
    keys_rot = (
        rotate(key_raw.reshape(local_rows, kv_heads, HD), offsets)
        .astype(jnp.bfloat16)
        .reshape(local_rows, kv_heads * HD)
    )
    kv_pairs = jnp.concatenate([keys_rot, values], axis=1)
    collect = lambda fold_keys, initial: gathered_keys(fold_keys, initial, kv_pairs)
    context = attend(queries, positions, block_starts, kv_heads, collect)
    return lax.psum_scatter(
        jnp.dot(context, w_out, preferred_element_type=jnp.float32).astype(jnp.bfloat16),
        "tp",
        scatter_dimension=0,
        tiled=True,
    )


def solution(mesh):
    placed = (P("seq", None), P(), P(None, "tp"), P(None, "tp"), P(None, "tp"), P("tp", None), P())
    return jax.shard_map(
        local, mesh=mesh, in_specs=placed, out_specs=P(("seq", "tp"), None), check_vma=False
    )
```

profile of v0, /device:TPU:96, one launch (start us, length us, event | category | flops | bytes accessed | tf_op | source)
XLA Modules:
  0.0 1441.7 jit_solution(14955877391649127810)
XLA Ops:
  26.3 50.0 %all-gather.2.cloned.1.call-done = bf16[8192,256]{0,1:T(8,128)(2,1)} async-done(((bf16[512,256]{0,1:T(8,128)(2,1)}), bf16[8192,256]{0,1:T(8,128)(2,1)}) %all-gather.2.cloned.1.call-update) | async-done | bytes 4194320 | tf_op jit(solution)/shard_map/all_gather | solution.py:53
  86.9 1203.8 %while.59 = (s32[]{:T(128)}, f32[4,1,512]{2,1,0:T(1,128)S(1)}, f32[4,1,512]{2,1,0:T(1,128)S(1)}, f32[4,1,512,128]{3,2,1,0:T(8,128)S(1)}, bf16[64,128,1,128]{3,1,...) while((s32[]{:T(128)}, f32[4,1,512]{2,1,0:T(1,128)S(1)}, ...), condition=%wide.region_13.14_spmd.clone.clone, body=%wide.region_3.13_spmd.clone.clone.sunk | while | flops 34936500 | bytes 2280639 | solution.py:137
  239.8 30.9 %while.60 = (s32[]{:T(128)}, f32[4,1,512]{2,1,0:T(1,128)S(1)}, f32[4,1,512]{2,1,0:T(1,128)S(1)}, f32[4,1,512,128]{3,2,1,0:T(8,128)S(1)}, s32[]{:T(128)}, /*index...) while((s32[]{:T(128)}, f32[4,1,512]{2,1,0:T(1,128)S(1)}, ...), condition=%wide.region_12.12_spmd.clone.clone, body=%wide.region_4.11_spmd.clone.clone.sunk | while | flops 34934960 | bytes 2093978 | solution.py:135
  272.1 30.9 %while.60 = (s32[]{:T(128)}, f32[4,1,512]{2,1,0:T(1,128)S(1)}, f32[4,1,512]{2,1,0:T(1,128)S(1)}, f32[4,1,512,128]{3,2,1,0:T(8,128)S(1)}, s32[]{:T(128)}, /*index...) while((s32[]{:T(128)}, f32[4,1,512]{2,1,0:T(1,128)S(1)}, ...), condition=%wide.region_12.12_spmd.clone.clone, body=%wide.region_4.11_spmd.clone.clone.sunk | while | flops 34934960 | bytes 2093978 | solution.py:135
  304.5 30.9 %while.60 = (s32[]{:T(128)}, f32[4,1,512]{2,1,0:T(1,128)S(1)}, f32[4,1,512]{2,1,0:T(1,128)S(1)}, f32[4,1,512,128]{3,2,1,0:T(8,128)S(1)}, s32[]{:T(128)}, /*index...) while((s32[]{:T(128)}, f32[4,1,512]{2,1,0:T(1,128)S(1)}, ...), condition=%wide.region_12.12_spmd.clone.clone, body=%wide.region_4.11_spmd.clone.clone.sunk | while | flops 34934960 | bytes 2093978 | solution.py:135
  336.9 30.9 %while.60 = (s32[]{:T(128)}, f32[4,1,512]{2,1,0:T(1,128)S(1)}, f32[4,1,512]{2,1,0:T(1,128)S(1)}, f32[4,1,512,128]{3,2,1,0:T(8,128)S(1)}, s32[]{:T(128)}, /*index...) while((s32[]{:T(128)}, f32[4,1,512]{2,1,0:T(1,128)S(1)}, ...), condition=%wide.region_12.12_spmd.clone.clone, body=%wide.region_4.11_spmd.clone.clone.sunk | while | flops 34934960 | bytes 2093978 | solution.py:135
  369.3 30.9 %while.60 = (s32[]{:T(128)}, f32[4,1,512]{2,1,0:T(1,128)S(1)}, f32[4,1,512]{2,1,0:T(1,128)S(1)}, f32[4,1,512,128]{3,2,1,0:T(8,128)S(1)}, s32[]{:T(128)}, /*index...) while((s32[]{:T(128)}, f32[4,1,512]{2,1,0:T(1,128)S(1)}, ...), condition=%wide.region_12.12_spmd.clone.clone, body=%wide.region_4.11_spmd.clone.clone.sunk | while | flops 34934960 | bytes 2093978 | solution.py:135
  401.6 30.9 %while.60 = (s32[]{:T(128)}, f32[4,1,512]{2,1,0:T(1,128)S(1)}, f32[4,1,512]{2,1,0:T(1,128)S(1)}, f32[4,1,512,128]{3,2,1,0:T(8,128)S(1)}, s32[]{:T(128)}, /*index...) while((s32[]{:T(128)}, f32[4,1,512]{2,1,0:T(1,128)S(1)}, ...), condition=%wide.region_12.12_spmd.clone.clone, body=%wide.region_4.11_spmd.clone.clone.sunk | while | flops 34934960 | bytes 2093978 | solution.py:135
  434.0 30.9 %while.60 = (s32[]{:T(128)}, f32[4,1,512]{2,1,0:T(1,128)S(1)}, f32[4,1,512]{2,1,0:T(1,128)S(1)}, f32[4,1,512,128]{3,2,1,0:T(8,128)S(1)}, s32[]{:T(128)}, /*index...) while((s32[]{:T(128)}, f32[4,1,512]{2,1,0:T(1,128)S(1)}, ...), condition=%wide.region_12.12_spmd.clone.clone, body=%wide.region_4.11_spmd.clone.clone.sunk | while | flops 34934960 | bytes 2093978 | solution.py:135
  466.4 30.9 %while.60 = (s32[]{:T(128)}, f32[4,1,512]{2,1,0:T(1,128)S(1)}, f32[4,1,512]{2,1,0:T(1,128)S(1)}, f32[4,1,512,128]{3,2,1,0:T(8,128)S(1)}, s32[]{:T(128)}, /*index...) while((s32[]{:T(128)}, f32[4,1,512]{2,1,0:T(1,128)S(1)}, ...), condition=%wide.region_12.12_spmd.clone.clone, body=%wide.region_4.11_spmd.clone.clone.sunk | while | flops 34934960 | bytes 2093978 | solution.py:135
  498.7 30.9 %while.60 = (s32[]{:T(128)}, f32[4,1,512]{2,1,0:T(1,128)S(1)}, f32[4,1,512]{2,1,0:T(1,128)S(1)}, f32[4,1,512,128]{3,2,1,0:T(8,128)S(1)}, s32[]{:T(128)}, /*index...) while((s32[]{:T(128)}, f32[4,1,512]{2,1,0:T(1,128)S(1)}, ...), condition=%wide.region_12.12_spmd.clone.clone, body=%wide.region_4.11_spmd.clone.clone.sunk | while | flops 34934960 | bytes 2093978 | solution.py:135
  531.1 30.9 %while.60 = (s32[]{:T(128)}, f32[4,1,512]{2,1,0:T(1,128)S(1)}, f32[4,1,512]{2,1,0:T(1,128)S(1)}, f32[4,1,512,128]{3,2,1,0:T(8,128)S(1)}, s32[]{:T(128)}, /*index...) while((s32[]{:T(128)}, f32[4,1,512]{2,1,0:T(1,128)S(1)}, ...), condition=%wide.region_12.12_spmd.clone.clone, body=%wide.region_4.11_spmd.clone.clone.sunk | while | flops 34934960 | bytes 2093978 | solution.py:135
  563.5 30.9 %while.60 = (s32[]{:T(128)}, f32[4,1,512]{2,1,0:T(1,128)S(1)}, f32[4,1,512]{2,1,0:T(1,128)S(1)}, f32[4,1,512,128]{3,2,1,0:T(8,128)S(1)}, s32[]{:T(128)}, /*index...) while((s32[]{:T(128)}, f32[4,1,512]{2,1,0:T(1,128)S(1)}, ...), condition=%wide.region_12.12_spmd.clone.clone, body=%wide.region_4.11_spmd.clone.clone.sunk | while | flops 34934960 | bytes 2093978 | solution.py:135
  595.9 30.9 %while.60 = (s32[]{:T(128)}, f32[4,1,512]{2,1,0:T(1,128)S(1)}, f32[4,1,512]{2,1,0:T(1,128)S(1)}, f32[4,1,512,128]{3,2,1,0:T(8,128)S(1)}, s32[]{:T(128)}, /*index...) while((s32[]{:T(128)}, f32[4,1,512]{2,1,0:T(1,128)S(1)}, ...), condition=%wide.region_12.12_spmd.clone.clone, body=%wide.region_4.11_spmd.clone.clone.sunk | while | flops 34934960 | bytes 2093978 | solution.py:135
  628.2 30.9 %while.60 = (s32[]{:T(128)}, f32[4,1,512]{2,1,0:T(1,128)S(1)}, f32[4,1,512]{2,1,0:T(1,128)S(1)}, f32[4,1,512,128]{3,2,1,0:T(8,128)S(1)}, s32[]{:T(128)}, /*index...) while((s32[]{:T(128)}, f32[4,1,512]{2,1,0:T(1,128)S(1)}, ...), condition=%wide.region_12.12_spmd.clone.clone, body=%wide.region_4.11_spmd.clone.clone.sunk | while | flops 34934960 | bytes 2093978 | solution.py:135
  660.6 30.9 %while.60 = (s32[]{:T(128)}, f32[4,1,512]{2,1,0:T(1,128)S(1)}, f32[4,1,512]{2,1,0:T(1,128)S(1)}, f32[4,1,512,128]{3,2,1,0:T(8,128)S(1)}, s32[]{:T(128)}, /*index...) while((s32[]{:T(128)}, f32[4,1,512]{2,1,0:T(1,128)S(1)}, ...), condition=%wide.region_12.12_spmd.clone.clone, body=%wide.region_4.11_spmd.clone.clone.sunk | while | flops 34934960 | bytes 2093978 | solution.py:135
  693.0 30.9 %while.60 = (s32[]{:T(128)}, f32[4,1,512]{2,1,0:T(1,128)S(1)}, f32[4,1,512]{2,1,0:T(1,128)S(1)}, f32[4,1,512,128]{3,2,1,0:T(8,128)S(1)}, s32[]{:T(128)}, /*index...) while((s32[]{:T(128)}, f32[4,1,512]{2,1,0:T(1,128)S(1)}, ...), condition=%wide.region_12.12_spmd.clone.clone, body=%wide.region_4.11_spmd.clone.clone.sunk | while | flops 34934960 | bytes 2093978 | solution.py:135
  725.3 30.9 %while.60 = (s32[]{:T(128)}, f32[4,1,512]{2,1,0:T(1,128)S(1)}, f32[4,1,512]{2,1,0:T(1,128)S(1)}, f32[4,1,512,128]{3,2,1,0:T(8,128)S(1)}, s32[]{:T(128)}, /*index...) while((s32[]{:T(128)}, f32[4,1,512]{2,1,0:T(1,128)S(1)}, ...), condition=%wide.region_12.12_spmd.clone.clone, body=%wide.region_4.11_spmd.clone.clone.sunk | while | flops 34934960 | bytes 2093978 | solution.py:135
  757.7 30.9 %while.60 = (s32[]{:T(128)}, f32[4,1,512]{2,1,0:T(1,128)S(1)}, f32[4,1,512]{2,1,0:T(1,128)S(1)}, f32[4,1,512,128]{3,2,1,0:T(8,128)S(1)}, s32[]{:T(128)}, /*index...) while((s32[]{:T(128)}, f32[4,1,512]{2,1,0:T(1,128)S(1)}, ...), condition=%wide.region_12.12_spmd.clone.clone, body=%wide.region_4.11_spmd.clone.clone.sunk | while | flops 34934960 | bytes 2093978 | solution.py:135
  790.1 30.9 %while.60 = (s32[]{:T(128)}, f32[4,1,512]{2,1,0:T(1,128)S(1)}, f32[4,1,512]{2,1,0:T(1,128)S(1)}, f32[4,1,512,128]{3,2,1,0:T(8,128)S(1)}, s32[]{:T(128)}, /*index...) while((s32[]{:T(128)}, f32[4,1,512]{2,1,0:T(1,128)S(1)}, ...), condition=%wide.region_12.12_spmd.clone.clone, body=%wide.region_4.11_spmd.clone.clone.sunk | while | flops 34934960 | bytes 2093978 | solution.py:135
  822.4 30.9 %while.60 = (s32[]{:T(128)}, f32[4,1,512]{2,1,0:T(1,128)S(1)}, f32[4,1,512]{2,1,0:T(1,128)S(1)}, f32[4,1,512,128]{3,2,1,0:T(8,128)S(1)}, s32[]{:T(128)}, /*index...) while((s32[]{:T(128)}, f32[4,1,512]{2,1,0:T(1,128)S(1)}, ...), condition=%wide.region_12.12_spmd.clone.clone, body=%wide.region_4.11_spmd.clone.clone.sunk | while | flops 34934960 | bytes 2093978 | solution.py:135
  854.8 30.9 %while.60 = (s32[]{:T(128)}, f32[4,1,512]{2,1,0:T(1,128)S(1)}, f32[4,1,512]{2,1,0:T(1,128)S(1)}, f32[4,1,512,128]{3,2,1,0:T(8,128)S(1)}, s32[]{:T(128)}, /*index...) while((s32[]{:T(128)}, f32[4,1,512]{2,1,0:T(1,128)S(1)}, ...), condition=%wide.region_12.12_spmd.clone.clone, body=%wide.region_4.11_spmd.clone.clone.sunk | while | flops 34934960 | bytes 2093978 | solution.py:135
  887.2 30.9 %while.60 = (s32[]{:T(128)}, f32[4,1,512]{2,1,0:T(1,128)S(1)}, f32[4,1,512]{2,1,0:T(1,128)S(1)}, f32[4,1,512,128]{3,2,1,0:T(8,128)S(1)}, s32[]{:T(128)}, /*index...) while((s32[]{:T(128)}, f32[4,1,512]{2,1,0:T(1,128)S(1)}, ...), condition=%wide.region_12.12_spmd.clone.clone, body=%wide.region_4.11_spmd.clone.clone.sunk | while | flops 34934960 | bytes 2093978 | solution.py:135
  919.6 30.9 %while.60 = (s32[]{:T(128)}, f32[4,1,512]{2,1,0:T(1,128)S(1)}, f32[4,1,512]{2,1,0:T(1,128)S(1)}, f32[4,1,512,128]{3,2,1,0:T(8,128)S(1)}, s32[]{:T(128)}, /*index...) while((s32[]{:T(128)}, f32[4,1,512]{2,1,0:T(1,128)S(1)}, ...), condition=%wide.region_12.12_spmd.clone.clone, body=%wide.region_4.11_spmd.clone.clone.sunk | while | flops 34934960 | bytes 2093978 | solution.py:135
  951.9 30.9 %while.60 = (s32[]{:T(128)}, f32[4,1,512]{2,1,0:T(1,128)S(1)}, f32[4,1,512]{2,1,0:T(1,128)S(1)}, f32[4,1,512,128]{3,2,1,0:T(8,128)S(1)}, s32[]{:T(128)}, /*index...) while((s32[]{:T(128)}, f32[4,1,512]{2,1,0:T(1,128)S(1)}, ...), condition=%wide.region_12.12_spmd.clone.clone, body=%wide.region_4.11_spmd.clone.clone.sunk | while | flops 34934960 | bytes 2093978 | solution.py:135
  984.3 30.9 %while.60 = (s32[]{:T(128)}, f32[4,1,512]{2,1,0:T(1,128)S(1)}, f32[4,1,512]{2,1,0:T(1,128)S(1)}, f32[4,1,512,128]{3,2,1,0:T(8,128)S(1)}, s32[]{:T(128)}, /*index...) while((s32[]{:T(128)}, f32[4,1,512]{2,1,0:T(1,128)S(1)}, ...), condition=%wide.region_12.12_spmd.clone.clone, body=%wide.region_4.11_spmd.clone.clone.sunk | while | flops 34934960 | bytes 2093978 | solution.py:135
  1016.7 30.9 %while.60 = (s32[]{:T(128)}, f32[4,1,512]{2,1,0:T(1,128)S(1)}, f32[4,1,512]{2,1,0:T(1,128)S(1)}, f32[4,1,512,128]{3,2,1,0:T(8,128)S(1)}, s32[]{:T(128)}, /*index...) while((s32[]{:T(128)}, f32[4,1,512]{2,1,0:T(1,128)S(1)}, ...), condition=%wide.region_12.12_spmd.clone.clone, body=%wide.region_4.11_spmd.clone.clone.sunk | while | flops 34934960 | bytes 2093978 | solution.py:135
  1049.0 30.9 %while.60 = (s32[]{:T(128)}, f32[4,1,512]{2,1,0:T(1,128)S(1)}, f32[4,1,512]{2,1,0:T(1,128)S(1)}, f32[4,1,512,128]{3,2,1,0:T(8,128)S(1)}, s32[]{:T(128)}, /*index...) while((s32[]{:T(128)}, f32[4,1,512]{2,1,0:T(1,128)S(1)}, ...), condition=%wide.region_12.12_spmd.clone.clone, body=%wide.region_4.11_spmd.clone.clone.sunk | while | flops 34934960 | bytes 2093978 | solution.py:135
  1081.4 30.9 %while.60 = (s32[]{:T(128)}, f32[4,1,512]{2,1,0:T(1,128)S(1)}, f32[4,1,512]{2,1,0:T(1,128)S(1)}, f32[4,1,512,128]{3,2,1,0:T(8,128)S(1)}, s32[]{:T(128)}, /*index...) while((s32[]{:T(128)}, f32[4,1,512]{2,1,0:T(1,128)S(1)}, ...), condition=%wide.region_12.12_spmd.clone.clone, body=%wide.region_4.11_spmd.clone.clone.sunk | while | flops 34934960 | bytes 2093978 | solution.py:135
  1113.8 30.9 %while.60 = (s32[]{:T(128)}, f32[4,1,512]{2,1,0:T(1,128)S(1)}, f32[4,1,512]{2,1,0:T(1,128)S(1)}, f32[4,1,512,128]{3,2,1,0:T(8,128)S(1)}, s32[]{:T(128)}, /*index...) while((s32[]{:T(128)}, f32[4,1,512]{2,1,0:T(1,128)S(1)}, ...), condition=%wide.region_12.12_spmd.clone.clone, body=%wide.region_4.11_spmd.clone.clone.sunk | while | flops 34934960 | bytes 2093978 | solution.py:135
  1146.2 24.6 %while.60 = (s32[]{:T(128)}, f32[4,1,512]{2,1,0:T(1,128)S(1)}, f32[4,1,512]{2,1,0:T(1,128)S(1)}, f32[4,1,512,128]{3,2,1,0:T(8,128)S(1)}, s32[]{:T(128)}, /*index...) while((s32[]{:T(128)}, f32[4,1,512]{2,1,0:T(1,128)S(1)}, ...), condition=%wide.region_12.12_spmd.clone.clone, body=%wide.region_4.11_spmd.clone.clone.sunk | while | flops 34934960 | bytes 2093978 | solution.py:135
  1297.9 137.0 %reduce-scatter.2.cloned.1.call-done = bf16[64,4096]{1,0:T(8,128)(2,1)} async-done(((bf16[512,4096]{1,0:T(8,128)(2,1)}), bf16[64,4096]{1,0:T(8,128)(2,1)}) %reduce-scatter.2.cloned.1.call-update) | async-done | bytes 524304 | tf_op jit(solution)/shard_map/reduce_scatter | solution.py:173
  (2526 shorter events, 2012.6 us)
Async XLA Ops:
  6.5 4.2 copy-start
  6.5 4.2 copy-start.3
  6.5 69.8 %all-gather.2.cloned.1.call-start = ((), (), s32[]{:S(2)}) async-start(), calls=%async_computation.1 | async-start | bytes 4456448 | tf_op jit(solution)/shard_map/all_gather | solution.py:53
  10.7 4.0 copy-start.1
  10.8 4.0 copy-start.2
  17.7 1417.1 %reduce-scatter.2.cloned.1.call-start = ((), (), s32[]{:S(2)}) async-start(), calls=%async_computation.2 | async-start | bytes 4718592 | tf_op jit(solution)/shard_map/reduce_scatter | solution.py:173
Sparse Core Ops, SparseCore 0:
  17.8 58.4 all-gather.1
  1298.0 136.7 reduce-scatter.1
where the time goes:
time: 1460 us; the launch traced here: 1440 us
  other arithmetic  683 us (47%)
  matrix products  257 us (18%)
  loops' own time  197 us (13%)
  waiting for transfers between devices  187 us (13%)
  local copies, waits for them, and re-layouts  104 us (7%)
    another operation x237, other arithmetic  328 us
    another operation x64, loops' own time, over_keys(): return lax.fori_loop(0, groups, over_groups, running)  183 us
    reduce_or x256, other arithmetic, over_groups(): jnp.any((block_first + key_width > tok_start[group_index]) & (block_first...  181 us
    reduce_scatter x1, waiting for transfers between devices, local(): lax.psum_scatter(jnp.dot(context, w_out, preferred_element_type=jnp.float...  137 us
    dot_general x118, matrix products, update(): jnp.einsum('hrd,khd->hrk', query_block, key_block, preferred_element_type...  133 us
    dot_general x118, matrix products, update(): jnp.einsum('hrk,khd->hrd', weights.astype(jnp.bfloat16), value_block, pre...  106 us
    scatter x118, other arithmetic, update(): totals.at[group_index].set(new_total)  74.8 us
    scatter x118, other arithmetic, update(): maxima.at[group_index].set(new_max)  74.2 us
  transfers between devices with their start and end apart: 2, of which 2 were waited for; matrix products, arithmetic and copies ran while one was open for 1% of the time, Pallas kernels for 0%

commit v1 on v0

v1 whole, which is shorter than its diff:
```python
import functools
import math

import jax
import jax.numpy as jnp
import numpy as np
from jax import lax
from jax.experimental import pallas as pl
from jax.experimental.pallas import tpu as pltpu
from jax.sharding import PartitionSpec as P

HD = 128
BLK = 128
ROWS = 512
BLOCKS = ROWS // BLK
HEADS = 4
REACH = 9
FAR = -1e30
rope_base = 500000.0
norm_epsilon = 1e-05
SCALE = HD ** (-0.5) * math.log2(math.e)


def frequencies():
    half = HD // 2
    inverse = np.exp(np.arange(half, dtype=np.float32) * np.float32(-2.0 * math.log(rope_base) / HD))
    return np.concatenate([inverse, inverse])[None, :].astype(np.float32)


def norm_rows(tok_ref, gain_ref, normed_ref, step):
    rows = pl.ds(pl.multiple_of(step * 16, 16), 16)
    floats = tok_ref[rows, :].astype(jnp.float32)
    mean = jnp.mean(floats * floats, axis=-1, keepdims=True)
    normed_ref[rows, :] = (floats * lax.rsqrt(mean + norm_epsilon) * gain_ref[...]).astype(jnp.bfloat16)


def block_start(doc_ref, block):
    mine = doc_ref[block]

    def count(j, total):
        return total + (doc_ref[j] < mine).astype(jnp.int32)

    return lax.fori_loop(0, doc_ref.shape[0], count, jnp.int32(0), unroll=True) * BLK


def make_tables(doc_ref, freq_ref, cos_ref, sin_ref, shard):
    lane = lax.broadcasted_iota(jnp.int32, (BLK, HD), 1)
    row = lax.broadcasted_iota(jnp.int32, (BLK, HD), 0)
    for b in range(BLOCKS):
        block = shard * BLOCKS + b
        offset = row + (block * BLK - block_start(doc_ref, block))
        angle = offset.astype(jnp.float32) * freq_ref[...]
        rows = pl.ds(b * BLK, BLK)
        cos_ref[rows, :] = jnp.cos(angle)
        sine = jnp.sin(angle)
        sin_ref[rows, :] = jnp.where(lane < HD // 2, -sine, sine)


def rotated(raw, cos, sin):
    return raw * cos + pltpu.roll(raw, HD // 2, 1) * sin


def project_kv(normed_ref, wk_ref, wv_ref, cos_ref, sin_ref, k_ref, v_ref):
    for half in range(2):
        rows = pl.ds(half * 256, 256)
        weights = jnp.concatenate([wk_ref[...], wv_ref[...]], axis=1)
        raw = jnp.dot(normed_ref[rows, :], weights, preferred_element_type=jnp.float32)
        k_ref[rows, :] = rotated(raw[:, :HD], cos_ref[rows, :], sin_ref[rows, :]).astype(jnp.bfloat16)
        v_ref[rows, :] = raw[:, HD:].astype(jnp.bfloat16)


def project_q(normed_ref, wq_ref, cos_ref, sin_ref, q_ref):
    for half in range(2):
        rows = pl.ds(half * 256, 256)
        raw = jnp.dot(normed_ref[rows, :], wq_ref[...], preferred_element_type=jnp.float32)
        cos = cos_ref[rows, :] * SCALE
        sin = sin_ref[rows, :] * SCALE
        for h in range(HEADS):
            out = rotated(raw[:, h * HD:(h + 1) * HD], cos, sin).astype(jnp.bfloat16)
            for b in range(2):
                q_ref[half * 2 + b, h * BLK:(h + 1) * BLK, :] = out[b * BLK:(b + 1) * BLK]


def front_kernel(doc_ref, tok_ref, gain_ref, wq_ref, wk_ref, wv_ref, freq_ref, q_ref, kv_ref, normed_ref, cos_ref, sin_ref):
    shard = lax.axis_index("seq")
    lax.fori_loop(0, ROWS // 16, lambda i, c: (norm_rows(tok_ref, gain_ref, normed_ref, i), c)[1], 0, unroll=2)
    make_tables(doc_ref, freq_ref, cos_ref, sin_ref, shard)
    project_kv(normed_ref, wk_ref, wv_ref, cos_ref, sin_ref, kv_ref.at[:, :HD], kv_ref.at[:, HD:])
    project_q(normed_ref, wq_ref, cos_ref, sin_ref, q_ref)


def query_marks(doc_ref, block):
    lane = lax.broadcasted_iota(jnp.int32, (HEADS * BLK, HD), 1)
    return (lane == doc_ref[block]).astype(jnp.bfloat16)


def key_marks(doc_ref, shard):
    lane = lax.broadcasted_iota(jnp.int32, (BLK, HD), 1)
    return jnp.concatenate(
        [
            jnp.where(lane == doc_ref[shard * BLOCKS + b], 0.0, FAR).astype(jnp.bfloat16)
            for b in range(BLOCKS)
        ],
        axis=0,
    )


def fold(q, keys, values, m_ref, acc_ref, i, rows, first):
    scores = lax.dot_general(q, keys, (((1,), (1,)), ((), ())), preferred_element_type=jnp.float32)
    if first is not None:
        count = scores.shape[0]
        token = lax.broadcasted_iota(jnp.int32, scores.shape, 0) % BLK + first
        key = lax.broadcasted_iota(jnp.int32, scores.shape, 1)
        scores = jnp.where(key <= token, scores, FAR)
        top = jnp.max(scores, axis=1, keepdims=True)
        weights = jnp.exp2(scores - top).astype(jnp.bfloat16)
        acc_ref[i, rows, :] = jnp.dot(weights, values, preferred_element_type=jnp.float32)
        m_ref[i, rows, :] = jnp.broadcast_to(top, (count, HD))
        return
    old = m_ref[i, rows, :]
    new = jnp.maximum(old, jnp.max(scores, axis=1, keepdims=True))
    weights = jnp.exp2(scores - new[:, :1]).astype(jnp.bfloat16)
    factor = jnp.exp2(old - new)
    product = jnp.dot(weights, values, preferred_element_type=jnp.float32)
    acc_ref[i, rows, :] = acc_ref[i, rows, :] * jnp.concatenate([factor, factor], axis=1) + product
    m_ref[i, rows, :] = new


def fold_own(q_ref, marks_ref, keys, values, m_ref, acc_ref):
    for i in range(BLOCKS):
        width = (i + 1) * BLK
        for c in range(2):
            rows = pl.ds(c * 256, 256)
            q = jnp.concatenate([q_ref[i, rows, :], marks_ref[i, rows, :]], axis=1)
            fold(q, keys[:width], values[:width], m_ref, acc_ref, i, rows, i * BLK)


def fold_shard(q_ref, marks_ref, keys, values, m_ref, acc_ref):
    def one(i, carry):
        for c in range(2):
            rows = pl.ds(c * 256, 256)
            q = jnp.concatenate([q_ref[i, rows, :], marks_ref[i, rows, :]], axis=1)
            fold(q, keys, values, m_ref, acc_ref, i, rows, None)
        return carry

    lax.fori_loop(0, BLOCKS, one, 0)


def context_of(acc_ref, i):
    heads = []
    for h in range(HEADS):
        acc = acc_ref[i, h * BLK:(h + 1) * BLK, :]
        heads.append((acc[:, :HD] / acc[:, HD:]).astype(jnp.bfloat16))
    return jnp.concatenate(heads, axis=1)


def back_kernel(doc_ref, q_ref, kv_ref, wo_ref, out_ref, marks_ref, m_ref, acc_ref):
    shard = lax.axis_index("seq")
    for i in range(BLOCKS):
        marks_ref[i] = query_marks(doc_ref, shard * BLOCKS + i)
    ones = jnp.ones((ROWS, HD), jnp.bfloat16)

    def pair(source):
        keys = jnp.concatenate([kv_ref[source, :, :HD], key_marks(doc_ref, source)], axis=1)
        values = jnp.concatenate([kv_ref[source, :, HD:], ones], axis=1)
        return keys, values

    fold_own(q_ref, marks_ref, *pair(shard), m_ref, acc_ref)

    def other(k, carry):
        fold_shard(q_ref, marks_ref, *pair(shard - k), m_ref, acc_ref)
        return carry

    lax.fori_loop(1, jnp.minimum(shard, REACH) + 1, other, 0)

    def project(i, carry):
        rows = pl.ds(pl.multiple_of(i * BLK, BLK), BLK)
        out_ref[rows, :] = jnp.dot(
            context_of(acc_ref, i), wo_ref[...], preferred_element_type=jnp.float32
        ).astype(jnp.bfloat16)
        return carry

    lax.fori_loop(0, BLOCKS, project, 0)


def local(tokens, norm_gain, w_query, w_key, w_value, w_out, doc_ids):
    vmem = pl.BlockSpec(memory_space=pltpu.VMEM)
    smem = pl.BlockSpec(memory_space=pltpu.SMEM)
    params = pltpu.CompilerParams(vmem_limit_bytes=56 * 2**20)
    queries, kv = pl.pallas_call(
        front_kernel,
        out_shape=(
            jax.ShapeDtypeStruct((BLOCKS, HEADS * BLK, HD), jnp.bfloat16),
            jax.ShapeDtypeStruct((ROWS, 2 * HD), jnp.bfloat16),
        ),
        in_specs=[smem] + [vmem] * 6,
        out_specs=(vmem, vmem),
        scratch_shapes=[
            pltpu.VMEM((ROWS, tokens.shape[1]), jnp.bfloat16),
            pltpu.VMEM((ROWS, HD), jnp.float32),
            pltpu.VMEM((ROWS, HD), jnp.float32),
        ],
        compiler_params=params,
    )(doc_ids, tokens, norm_gain[None, :], w_query, w_key, w_value, jnp.asarray(frequencies()))
    gathered = lax.all_gather(kv, "seq", axis=0, tiled=False)
    partial = pl.pallas_call(
        back_kernel,
        out_shape=jax.ShapeDtypeStruct((ROWS, w_out.shape[1]), jnp.bfloat16),
        in_specs=[smem] + [vmem] * 3,
        out_specs=vmem,
        scratch_shapes=[
            pltpu.VMEM((BLOCKS, HEADS * BLK, HD), jnp.bfloat16),
            pltpu.VMEM((BLOCKS, HEADS * BLK, HD), jnp.float32),
            pltpu.VMEM((BLOCKS, HEADS * BLK, 2 * HD), jnp.float32),
        ],
        compiler_params=params,
    )(doc_ids, queries, gathered, w_out)
    return lax.psum_scatter(partial, "tp", scatter_dimension=0, tiled=True)


def solution(mesh):
    placed = (P("seq", None), P(), P(None, "tp"), P(None, "tp"), P(None, "tp"), P("tp", None), P())
    return jax.shard_map(
        local, mesh=mesh, in_specs=placed, out_specs=P(("seq", "tp"), None), check_vma=False
    )
```

time: 1460 us -> 162 us (0.11); the launches traced: 1440 us -> 161 us
  other arithmetic: 683 us -> 0 us
  matrix products: 257 us -> 0 us
  loops' own time: 197 us -> 0 us
  local copies, waits for them, and re-layouts: 104 us -> 0 us
  waiting for transfers between devices: 187 us -> 90.7 us
  Pallas kernels: 0 us -> 56.8 us
    another operation x237 -> x0, other arithmetic: 328 us -> none
    dot_general x240 -> x0, matrix products: 257 us -> none  [the longest x118 133 us: update(): jnp.einsum('hrd,khd->hrk', query_block, key_block, preferred_element_type...]
    another operation x321 -> x0, loops' own time: 197 us -> none  [the longest x64 183 us: over_keys(): return lax.fori_loop(0, groups, over_groups, running)]
    reduce_or x256 -> x0, other arithmetic: 181 us -> none  [over_groups(): jnp.any((block_first + key_width > tok_start[group_index]) & (block_first...]
    scatter x236 -> x0, other arithmetic: 149 us -> none  [the longest x118 74.8 us: update(): totals.at[group_index].set(new_total)]
    reduce_scatter x1, waiting for transfers between devices: 137 us -> 37.8 us  [local(): return lax.psum_scatter(partial, 'tp', scatter_dimension=0, tiled=True)]
    pallas_call x0 -> x2, Pallas kernels: none -> 56.8 us  [the longest x1 44.7 us: local(): pl.pallas_call(back_kernel, out_shape=jax.ShapeDtypeStruct((ROWS, w_out.s...]
    squeeze x64 -> x0, local copies, waits for them, and re-layouts: 50.4 us -> none  [over_keys(): lax.dynamic_index_in_dim(value_split, key_step, 0, keepdims=False)]
  transfers between devices with their start and end apart: 2 -> 2, of which waited for: 2 -> 2; matrix products, arithmetic and copies ran while one was open for 1% -> 0% of each run, Pallas kernels for 0% -> 0%
where the time goes in v1:
time: 162 us; the launch traced here: 161 us
  waiting for transfers between devices  90.7 us (56%)
  Pallas kernels  56.8 us (35%)
  between operations  13.4 us (8%)
    all_gather x1, waiting for transfers between devices, local(): gathered = lax.all_gather(kv, 'seq', axis=0, tiled=False)  52.9 us
    pallas_call x1, Pallas kernels, local(): pl.pallas_call(back_kernel, out_shape=jax.ShapeDtypeStruct((ROWS, w_out.s...  44.7 us
    reduce_scatter x1, waiting for transfers between devices, local(): return lax.psum_scatter(partial, 'tp', scatter_dimension=0, tiled=True)  37.8 us
    pallas_call x1, Pallas kernels, local(): pl.pallas_call(front_kernel, out_shape=(jax.ShapeDtypeStruct((BLOCKS, HEA...  12.1 us
  transfers between devices with their start and end apart: 2, of which 2 were waited for; matrix products, arithmetic and copies ran while one was open for 0% of the time, Pallas kernels for 0%

profile of v1, /device:TPU:96, one launch (start us, length us, event | category | flops | bytes accessed | tf_op | source)
XLA Modules:
  0.0 161.0 jit_solution(6074684340064529188)
XLA Ops:
  6.5 0.0 all-gather.3.cloned.1.call-start
  6.5 12.1 %shard_map.82 = (bf16[4,512,128]{2,1,0:T(8,128)(2,1)}, bf16[512,256]{1,0:T(8,128)(2,1)}) custom-call(s32[64]{0:T(128)} %doc_ref.3, bf16[512,4096]{1,0:T(8,128)(2,1)} %tok_ref.1, f32[1,4096]{1,0:T(1,128)} %bitcast.3, bf16[4096,512]{1,0:T(8,128)(2,1)} %wq_ref.1, bf16[4096,128]{1,0:T(8,128)(2,1)} %wk_ref.1, bf16[4096,128]{1,0:T(8,128)(2,1)} %wv_ref.1, ...), custom_call_target="tpu_custom_call" | custom-call | tf_op jit(solution)/shard_map/pallas_call | solution.py:190
  18.6 0.0 all-gather.3.cloned.1.call-update
  18.6 0.0 reduce-scatter.2.cloned.1.call-start
  18.7 52.9 %all-gather.3.cloned.1.call-done = bf16[8192,256]{1,0:T(8,128)(2,1)} async-done(((bf16[512,256]{1,0:T(8,128)(2,1)}), bf16[8192,256]{1,0:T(8,128)(2,1)}) %all-gather.3.cloned.1.call-update) | async-done | bytes 4194320 | tf_op jit(solution)/shard_map/all_gather | solution.py:205
  71.5 44.7 %shard_map.83 = bf16[512,4096]{1,0:T(8,128)(2,1)} custom-call(s32[64]{0:T(128)} %doc_ref.3, bf16[4,512,128]{2,1,0:T(8,128)(2,1)} %get-tuple-element.7.q_ref, bf16[16,512,256]{2,1,0:T(8,128)(2,1)} %bitcast.2, bf16[512,4096]{1,0:T(8,128)(2,1)} %wo_ref.1), custom_call_target="tpu_custom_call" | custom-call | tf_op jit(solution)/shard_map/pallas_call | solution.py:206
  116.3 0.0 reduce-scatter.2.cloned.1.call-update
  116.3 37.8 %reduce-scatter.2.cloned.1.call-done = bf16[64,4096]{1,0:T(8,128)(2,1)} async-done(((bf16[512,4096]{1,0:T(8,128)(2,1)}), bf16[64,4096]{1,0:T(8,128)(2,1)}) %reduce-scatter.2.cloned.1.call-update) | async-done | bytes 524304 | tf_op jit(solution)/shard_map/reduce_scatter | solution.py:218
Async XLA Ops:
  6.5 65.0 %all-gather.3.cloned.1.call-start = ((), (), s32[]{:S(2)}) async-start(), calls=%async_computation.2 | async-start | bytes 4456448 | tf_op jit(solution)/shard_map/all_gather | solution.py:205
  18.6 135.5 %reduce-scatter.2.cloned.1.call-start = ((), (), s32[]{:S(2)}) async-start(), calls=%async_computation.1 | async-start | bytes 4718592 | tf_op jit(solution)/shard_map/reduce_scatter | solution.py:218
Sparse Core Ops, SparseCore 0:
  18.8 52.7 all-gather.2
  116.4 37.6 reduce-scatter.1

commit v2 on v1

v2 whole, which is shorter than its diff:
```python
import math

import jax
import jax.numpy as jnp
import numpy as np
from jax import lax
from jax.experimental import pallas as pl
from jax.experimental.pallas import tpu as pltpu
from jax.sharding import PartitionSpec as P

HD = 128
BLK = 128
ROWS = 512
BLOCKS = ROWS // BLK
HEADS = 4
PIECES = 2
MESH = pl.DeviceIdType.MESH
FAR = -1e30
rope_base = 500000.0
norm_epsilon = 1e-05
SCALE = HD ** (-0.5) * math.log2(math.e)


def frequencies():
    half = HD // 2
    inverse = np.exp(np.arange(half, dtype=np.float32) * np.float32(-2.0 * math.log(rope_base) / HD))
    return np.concatenate([inverse, inverse])[None, :].astype(np.float32)


def norm_rows(tok_ref, gain_ref, normed_ref, step):
    rows = pl.ds(pl.multiple_of(step * 16, 16), 16)
    floats = tok_ref[rows, :].astype(jnp.float32)
    mean = jnp.mean(floats * floats, axis=-1, keepdims=True)
    normed_ref[rows, :] = (floats * lax.rsqrt(mean + norm_epsilon) * gain_ref[...]).astype(jnp.bfloat16)


def block_start(doc_ref, block):
    mine = doc_ref[block]

    def count(j, total):
        return total + (doc_ref[j] < mine).astype(jnp.int32)

    return lax.fori_loop(0, doc_ref.shape[0], count, jnp.int32(0), unroll=True) * BLK


def make_tables(doc_ref, freq_ref, cos_ref, sin_ref, shard):
    lane = lax.broadcasted_iota(jnp.int32, (BLK, HD), 1)
    row = lax.broadcasted_iota(jnp.int32, (BLK, HD), 0)

    def one(b, carry):
        block = shard * BLOCKS + b
        offset = row + (block * BLK - block_start(doc_ref, block))
        angle = offset.astype(jnp.float32) * freq_ref[...]
        rows = pl.ds(pl.multiple_of(b * BLK, BLK), BLK)
        cos_ref[rows, :] = jnp.cos(angle)
        sine = jnp.sin(angle)
        sin_ref[rows, :] = jnp.where(lane < HD // 2, -sine, sine)
        return carry

    lax.fori_loop(0, BLOCKS, one, 0)


def rotated(raw, cos, sin):
    return raw * cos + pltpu.roll(raw, HD // 2, 1) * sin


def project_kv(normed_ref, wkv_ref, cos_ref, sin_ref, kv_ref):
    for half in range(2):
        rows = pl.ds(half * 256, 256)
        raw = jnp.dot(normed_ref[rows, :], wkv_ref[...], preferred_element_type=jnp.float32)
        kv_ref[rows, :] = rotated(raw[:, :HD], cos_ref[rows, :], sin_ref[rows, :]).astype(jnp.bfloat16)
        for b in range(2):
            at = ROWS + (half * 2 + b) * BLK
            kv_ref[at:at + BLK, :] = raw[b * BLK:(b + 1) * BLK, HD:].T.astype(jnp.bfloat16)


def project_q(normed_ref, wq_ref, cos_ref, sin_ref, q_ref, doc_ref, shard):
    lane = lax.broadcasted_iota(jnp.int32, (HEADS * BLK, HD), 1)
    for half in range(2):
        rows = pl.ds(half * 256, 256)
        raw = jnp.dot(normed_ref[rows, :], wq_ref[...], preferred_element_type=jnp.float32)
        cos = cos_ref[rows, :] * SCALE
        sin = sin_ref[rows, :] * SCALE
        for h in range(HEADS):
            out = rotated(raw[:, h * HD:(h + 1) * HD], cos, sin).astype(jnp.bfloat16)
            for b in range(2):
                q_ref[half * 2 + b, h * BLK:(h + 1) * BLK, :HD] = out[b * BLK:(b + 1) * BLK]
    for i in range(BLOCKS):
        q_ref[i, :, HD:] = (lane == doc_ref[shard * BLOCKS + i]).astype(jnp.bfloat16)


def slot_pair(kv_ref, slot, doc_ref, shard):
    lane = lax.broadcasted_iota(jnp.int32, (BLK, HD), 1)
    marks = [
        jnp.where(lane == doc_ref[shard * BLOCKS + b], 0.0, FAR).astype(jnp.bfloat16)
        for b in range(BLOCKS)
    ]
    keys = jnp.concatenate([kv_ref[slot, :ROWS, :], jnp.concatenate(marks, axis=0)], axis=1)
    columns = [kv_ref[slot, ROWS + b * BLK:ROWS + (b + 1) * BLK, :] for b in range(BLOCKS)]
    values = jnp.concatenate(
        [jnp.concatenate(columns, axis=1), jnp.ones((16, ROWS), jnp.bfloat16)], axis=0
    )
    return keys, values


def scores_of(keys, q):
    return lax.dot_general(keys, q, (((1,), (1,)), ((), ())), preferred_element_type=jnp.float32)


def fold_own(q_ref, keys, values, m_ref, acc_ref):
    token = lax.broadcasted_iota(jnp.int32, (BLK, HEADS * BLK), 1) % BLK
    key = lax.broadcasted_iota(jnp.int32, (BLK, HEADS * BLK), 0)
    causal = key <= token
    for i in range(BLOCKS):
        width = (i + 1) * BLK
        scores = scores_of(keys[:width], q_ref[i])
        last = jnp.where(causal, scores[width - BLK:], FAR)
        scores = last if i == 0 else jnp.concatenate([scores[:width - BLK], last], axis=0)
        top = jnp.max(scores, axis=0, keepdims=True)
        weights = jnp.exp2(scores - top).astype(jnp.bfloat16)
        acc_ref[i] = jnp.dot(values[:, :width], weights, preferred_element_type=jnp.float32)
        m_ref[i, 0:1, :] = top


def fold_shard(q_ref, keys, values, m_ref, acc_ref):
    scores = scores_of(keys, q_ref[0])
    for i in range(BLOCKS):
        following = scores_of(keys, q_ref[i + 1]) if i + 1 < BLOCKS else None
        old = m_ref[i, 0:1, :]
        new = jnp.maximum(old, jnp.max(scores, axis=0, keepdims=True))
        weights = jnp.exp2(scores - new).astype(jnp.bfloat16)
        factor = jnp.exp2(old - new)
        product = jnp.dot(values, weights, preferred_element_type=jnp.float32)
        acc_ref[i] = acc_ref[i] * factor + product
        m_ref[i, 0:1, :] = new
        scores = following


def write_context(acc_ref, i, ctx_ref):
    for h in range(HEADS):
        columns = pl.ds(h * BLK, BLK)
        scaled = acc_ref[i, :HD, columns] / acc_ref[i, HD:HD + 1, columns]
        ctx_ref[:, columns] = scaled.T.astype(jnp.bfloat16)


def kernel(
    doc_ref, tok_hbm, gain_ref, wq_hbm, wk_hbm, wv_hbm, freq_ref, wo_hbm, out_ref,
    tok_ref, wkv_ref, wq_ref, wo_ref, normed_ref, cos_ref, sin_ref, q_ref, kv_ref, m_ref, acc_ref,
    ctx_ref, mine_ref, give_ref, take_ref, pass_ref, half_ref, last_ref,
    load_sem, kv_send, kv_recv, give_send, give_recv, pass_send, half_recv, last_recv,
):
    shard = lax.axis_index("seq")
    part = lax.axis_index("tp")
    z, y = shard // 4, shard % 4
    x, c = part // 2, part % 2

    def at_seq(zz, yy):
        return (((zz + 4) % 4) * 4 + (yy + 4) % 4, part)

    def at_tp(xx, cc):
        return (shard, ((xx + 4) % 4) * 2 + cc)

    loads = []
    for n in range(4):
        rows = pl.ds(n * BLK, BLK)
        loads.append(pltpu.make_async_copy(tok_hbm.at[rows, :], tok_ref.at[rows, :], load_sem.at[n]))
    loads.append(pltpu.make_async_copy(wk_hbm, wkv_ref.at[:, :HD], load_sem.at[4]))
    loads.append(pltpu.make_async_copy(wv_hbm, wkv_ref.at[:, HD:], load_sem.at[5]))
    loads.append(pltpu.make_async_copy(wq_hbm, wq_ref, load_sem.at[6]))
    loads.append(pltpu.make_async_copy(wo_hbm, wo_ref, load_sem.at[7]))
    for load in loads:
        load.start()

    barrier = pltpu.get_barrier_semaphore()
    near = [at_seq(z, y + 1), at_seq(z, y - 1), at_seq(z + 1, y), at_seq(z - 1, y)]
    near += [at_tp(x + 1, c), at_tp(x - 1, c), at_tp(x, 1 - c)]
    for device in near:
        pl.semaphore_signal(barrier, inc=1, device_id=device, device_id_type=MESH)
    first_corner = (z == 0) & (y == 3)
    last_corner = (z == 3) & (y == 0)

    @pl.when(first_corner)
    def _():
        pl.semaphore_signal(barrier, inc=1, device_id=(12, part), device_id_type=MESH)

    @pl.when(last_corner)
    def _():
        pl.semaphore_signal(barrier, inc=1, device_id=(3, part), device_id_type=MESH)

    make_tables(doc_ref, freq_ref, cos_ref, sin_ref, shard)
    for n in range(4):
        loads[n].wait()
        lax.fori_loop(n * 8, n * 8 + 8, lambda i, s: (norm_rows(tok_ref, gain_ref, normed_ref, i), s)[1], 0)
    loads[4].wait()
    loads[5].wait()
    own = y
    project_kv(normed_ref, wkv_ref, cos_ref, sin_ref, kv_ref.at[own])

    pl.semaphore_wait(barrier, len(near) + (first_corner | last_corner).astype(jnp.int32))

    def slot_of(j, step):
        return j * 4 + (y + step + 4) % 4

    def move(name, source, target, device, piece):
        rows = pl.ds(piece * (2 * ROWS // PIECES), 2 * ROWS // PIECES)
        return pltpu.make_async_remote_copy(
            src_ref=kv_ref.at[source, rows, :],
            dst_ref=kv_ref.at[target, rows, :],
            send_sem=kv_send.at[name * PIECES + piece],
            recv_sem=kv_recv.at[target * PIECES + piece],
            device_id=device,
            device_id_type=MESH,
        )

    up, down = at_seq(z, y + 1), at_seq(z, y - 1)
    onward = at_seq(z + 1, y)
    transfers = {}
    for j in range(3):
        transfers["right", j] = (j * 4, slot_of(j, 0), slot_of(j, 0), up)
        transfers["left", j] = (j * 4 + 1, slot_of(j, 0), slot_of(j, 0), down)
        transfers["pass right", j] = (j * 4 + 2, slot_of(j, -1), slot_of(j, -1), up)
        transfers["pass left", j] = (j * 4 + 3, slot_of(j, 1), slot_of(j, 1), down)
    transfers["onward", 0] = (12, slot_of(0, 0), slot_of(1, 0), onward)
    transfers["onward", 1] = (13, slot_of(1, 0), slot_of(2, 0), onward)
    transfers["corner", 0] = (14, slot_of(0, 0), 12, (12, part))
    sends = {
        ("right", 0): y <= 2, ("left", 0): y == 0, ("pass right", 0): y == 2, ("pass left", 0): y == 3,
        ("right", 1): z >= 1, ("left", 1): z >= 1, ("pass left", 1): z >= 1,
        ("right", 2): z >= 2, ("left", 2): (z >= 2) & (y >= 1),
        ("pass right", 2): (z >= 2) & (y == 3), ("pass left", 2): (z >= 2) & (y == 2),
        ("onward", 0): z <= 2, ("onward", 1): (z >= 1) & (z <= 2), ("corner", 0): first_corner,
    }
    arrives = {
        (0, -1): y >= 1, (0, 1): y == 3, (0, 2): y >= 2,
        (1, 0): z >= 1, (1, -1): z >= 1, (1, 1): z >= 1, (1, 2): z >= 1,
        (2, 0): z >= 2, (2, -1): z >= 2, (2, 1): (z >= 2) & (y <= 2), (2, 2): (z >= 2) & (y <= 1),
        (3, 0): last_corner,
    }

    def start(*keys):
        for key in keys:
            @pl.when(sends[key])
            def _(key=key):
                for piece in range(PIECES):
                    move(*transfers[key], piece).start()

    def arrive(key, *then):
        j, step = key
        slot = 12 if j == 3 else slot_of(j, step)

        @pl.when(arrives[key])
        def _():
            for piece in range(PIECES):
                move(0, slot, slot, up, piece).wait_recv()
                for other in then:
                    @pl.when(sends[other])
                    def _(other=other):
                        move(*transfers[other], piece).start()

    start(("onward", 0), ("right", 0), ("left", 0), ("corner", 0))
    loads[6].wait()
    project_q(normed_ref, wq_ref, cos_ref, sin_ref, q_ref, doc_ref, shard)
    fold_own(q_ref, *slot_pair(kv_ref, own, doc_ref, shard), m_ref, acc_ref)

    order = [
        ((0, -1), [((1, 0), ("onward", 1), ("right", 1), ("left", 1)), ((0, -1), ("pass right", 0))]),
        ((1, 0), [((0, 1), ("pass left", 0))]),
        ((0, 1), []),
        ((1, 1), [((2, 0), ("right", 2), ("left", 2)), ((1, 1), ("pass left", 1))]),
        ((0, 2), [((0, 2),)]),
        ((1, -1), [((1, -1),)]),
        ((2, 0), [((2, -1), ("pass right", 2)), ((2, 1), ("pass left", 2))]),
        ((2, -1), []),
        ((2, 1), []),
        ((1, 2), [((1, 2),)]),
        ((2, 2), [((2, 2),)]),
        ((3, 0), [((3, 0),)]),
    ]

    def step(k, carry):
        row, turn, valid = jnp.int32(0), jnp.int32(0), jnp.int32(0)
        for n, (key, events) in enumerate(order):
            if events:
                @pl.when(k == n)
                def _(events=events):
                    for event in events:
                        arrive(*event)
            here = k == n
            row = jnp.where(here, key[0], row)
            turn = jnp.where(here, (y + key[1] + 4) % 4, turn)
            valid = jnp.where(here, arrives[key].astype(jnp.int32), valid)
        corner = row == 3
        slot = jnp.where(corner, 12, row * 4 + turn)
        source = jnp.where(corner, 3, (z - row) * 4 + turn)

        @pl.when(valid == 1)
        def _():
            fold_shard(q_ref, *slot_pair(kv_ref, slot, doc_ref, source), m_ref, acc_ref)

        return carry

    lax.fori_loop(0, len(order), step, 0)
    for key in sends:
        @pl.when(sends[key])
        def _(key=key):
            for piece in range(PIECES):
                move(*transfers[key], piece).wait_send()

    loads[7].wait()
    half = wo_ref.shape[1] // 2

    def give(k):
        return pltpu.make_async_remote_copy(
            src_ref=give_ref.at[k], dst_ref=take_ref.at[k], send_sem=give_send.at[k], recv_sem=give_recv.at[k],
            device_id=at_tp(x, 1 - c), device_id_type=MESH,
        )

    def halves(h):
        return pltpu.make_async_remote_copy(
            src_ref=pass_ref.at[0, h], dst_ref=half_ref.at[h], send_sem=pass_send.at[h], recv_sem=half_recv.at[h],
            device_id=at_tp(x + 1 - 2 * h, c), device_id_type=MESH,
        )

    def lasts(k):
        return pltpu.make_async_remote_copy(
            src_ref=pass_ref.at[k], dst_ref=last_ref.at[k - 1], send_sem=pass_send.at[1 + k], recv_sem=last_recv.at[k - 1],
            device_id=at_tp(x + 3 - 2 * k, c), device_id_type=MESH,
        )

    def project(k, carry):
        i = jnp.where(k == 0, x + 2, jnp.where(k == 1, x + 1, jnp.where(k == 2, x + 3, x))) % 4
        write_context(acc_ref, i, ctx_ref)
        theirs = ctx_ref[pl.ds(pl.multiple_of((1 - c) * 64, 64), 64), :]
        ours = ctx_ref[pl.ds(pl.multiple_of(c * 64, 64), 64), :]
        both = jnp.concatenate([theirs, ours], axis=0)
        product = jnp.dot(both, wo_ref[...], preferred_element_type=jnp.float32)
        for h in range(2):
            columns = slice(h * half, (h + 1) * half)
            give_ref[k, h] = product[:64, columns].astype(jnp.bfloat16)
            mine_ref[k, h] = product[64:, columns]
        give(k).start()
        return carry

    def paired(k, h):
        return mine_ref[k, h] + take_ref[k, h].astype(jnp.float32)

    lax.fori_loop(0, 2, project, 0)
    give(0).wait_recv()
    for h in range(2):
        pass_ref[0, h] = paired(0, h).astype(jnp.bfloat16)
        halves(h).start()
    lax.fori_loop(2, 4, project, 0)
    for k in (1, 2):
        give(k).wait_recv()
        halves(k - 1).wait_recv()
        for h in range(2):
            total = paired(k, h)
            if h == k - 1:
                total = total + half_ref[h].astype(jnp.float32)
            pass_ref[k, h] = total.astype(jnp.bfloat16)
        lasts(k).start()
    give(3).wait_recv()
    for h in range(2):
        mine_ref[3, h] = paired(3, h)
    lasts(1).wait_recv()
    lasts(2).wait_recv()
    for h in range(2):
        total = mine_ref[3, h] + last_ref[0, h].astype(jnp.float32) + last_ref[1, h].astype(jnp.float32)
        out_ref[:, h * half:(h + 1) * half] = total.astype(jnp.bfloat16)
    for k in range(4):
        give(k).wait_send()
    for h in range(2):
        halves(h).wait_send()
        lasts(h + 1).wait_send()


def local(tokens, norm_gain, w_query, w_key, w_value, w_out, doc_ids):
    vmem = pl.BlockSpec(memory_space=pltpu.VMEM)
    smem = pl.BlockSpec(memory_space=pltpu.SMEM)
    hbm = pl.BlockSpec(memory_space=pl.ANY)
    width = tokens.shape[1]
    half = w_out.shape[1] // 2
    b16, f32 = jnp.bfloat16, jnp.float32
    dma = pltpu.SemaphoreType.DMA
    return pl.pallas_call(
        kernel,
        out_shape=jax.ShapeDtypeStruct((64, w_out.shape[1]), b16),
        in_specs=[smem, hbm, vmem, hbm, hbm, hbm, vmem, hbm],
        out_specs=vmem,
        scratch_shapes=[
            pltpu.VMEM((ROWS, width), b16),
            pltpu.VMEM((width, 2 * HD), b16),
            pltpu.VMEM((width, HEADS * HD), b16),
            pltpu.VMEM((HEADS * HD, w_out.shape[1]), b16),
            pltpu.VMEM((ROWS, width), b16),
            pltpu.VMEM((ROWS, HD), f32),
            pltpu.VMEM((ROWS, HD), f32),
            pltpu.VMEM((BLOCKS, HEADS * BLK, 2 * HD), b16),
            pltpu.VMEM((13, 2 * ROWS, HD), b16),
            pltpu.VMEM((BLOCKS, 8, HEADS * BLK), f32),
            pltpu.VMEM((BLOCKS, HD + 16, HEADS * BLK), f32),
            pltpu.VMEM((BLK, HEADS * HD), b16),
            pltpu.VMEM((4, 2, 64, half), f32),
            pltpu.VMEM((4, 2, 64, half), b16),
            pltpu.VMEM((4, 2, 64, half), b16),
            pltpu.VMEM((3, 2, 64, half), b16),
            pltpu.VMEM((2, 64, half), b16),
            pltpu.VMEM((2, 2, 64, half), b16),
            dma((8,)), dma((15 * PIECES,)), dma((13 * PIECES,)), dma((4,)), dma((4,)), dma((4,)), dma((2,)), dma((2,)),
        ],
        compiler_params=pltpu.CompilerParams(
            vmem_limit_bytes=58 * 2**20, collective_id=0, has_side_effects=True
        ),
        cost_estimate=pl.CostEstimate(flops=10**10, bytes_accessed=15 * 2**20, transcendentals=10**7),
    )(doc_ids, tokens, norm_gain[None, :], w_query, w_key, w_value, jnp.asarray(frequencies()), w_out)


def solution(mesh):
    placed = (P("seq", None), P(), P(None, "tp"), P(None, "tp"), P(None, "tp"), P("tp", None), P())
    return jax.shard_map(
        local, mesh=mesh, in_specs=placed, out_specs=P(("seq", "tp"), None), check_vma=False
    )
```

time: 162 us -> 71.3 us (0.44)
  waiting for transfers between devices: 90.7 us -> 0 us
  between operations: 13.4 us -> 0.01 us
  Pallas kernels: 56.8 us -> 69.2 us
  local copies, waits for them, and re-layouts: 0 us -> 1.87 us
    all_gather x1 -> x0, waiting for transfers between devices: 52.9 us -> none  [local(): gathered = lax.all_gather(kv, 'seq', axis=0, tiled=False)]
    reduce_scatter x1 -> x0, waiting for transfers between devices: 37.8 us -> none  [local(): return lax.psum_scatter(partial, 'tp', scatter_dimension=0, tiled=True)]
    pallas_call x2 -> x1, Pallas kernels: 56.8 us -> 69.2 us  [local(): pl.pallas_call(kernel, out_shape=jax.ShapeDtypeStruct((64, w_out.shape[1]...]
    unnamed x0 -> x1, local copies, waits for them, and re-layouts: none -> 1.87 us
  transfers between devices with their start and end apart: 2 -> 0, of which waited for: 2 -> 0; matrix products, arithmetic and copies ran while one was open for 0% -> 0% of each run, Pallas kernels for 0% -> 0%
where the time goes in v2:
time: 71.3 us; the launch traced here: 71.1 us
  Pallas kernels  69.2 us (97%)
  local copies, waits for them, and re-layouts  1.87 us (3%)
    pallas_call x1, Pallas kernels, local(): pl.pallas_call(kernel, out_shape=jax.ShapeDtypeStruct((64, w_out.shape[1]...  69.2 us
    unnamed x1, local copies, waits for them, and re-layouts  1.87 us

profile of v2, /device:TPU:96, one launch (start us, length us, event | category | flops | bytes accessed | tf_op | source)
XLA Modules:
  0.0 71.1 jit_solution(2545144337615294913)
XLA Ops:
  0.0 69.2 %shard_map.82 = bf16[64,4096]{1,0:T(8,128)(2,1)} custom-call(s32[64]{0:T(128)} %doc_ref.1, bf16[512,4096]{1,0:T(8,128)(2,1)} %tok_hbm.1, f32[1,4096]{1,0:T(1,128)} %bitcast.1, bf16[4096,512]{1,0:T(8,128)(2,1)} %wq_hbm.1, bf16[4096,128]{1,0:T(8,128)(2,1)} %wk_hbm.1, bf16[4096,128]{1,0:T(8,128)(2,1)} %wv_hbm.1, f32[1,128]{1,0:T(1,128)} %constant.2.clone.freq_ref, ...), custom_call_target="tpu_custom_call" | custom-call | flops 10000000000 | bytes 15728640 | tf_op jit(solution)/shard_map/pallas_call | solution.py:385
  69.2 1.9 %copy.10 = bf16[64,4096]{1,0:T(8,128)(2,1)} copy(bf16[64,4096]{1,0:T(8,128)(2,1)} %shard_map.82) | data formatting | bytes 1048576

commit v3 on v2

--- a/solution.py
+++ b/solution.py
@@ -14,6 +14,7 @@
 BLOCKS = ROWS // BLK
 HEADS = 4
 PIECES = 2
+NORM_ROWS = 32
 MESH = pl.DeviceIdType.MESH
 FAR = -1e30
 rope_base = 500000.0
@@ -28,10 +29,17 @@
 
 
 def norm_rows(tok_ref, gain_ref, normed_ref, step):
-    rows = pl.ds(pl.multiple_of(step * 16, 16), 16)
-    floats = tok_ref[rows, :].astype(jnp.float32)
-    mean = jnp.mean(floats * floats, axis=-1, keepdims=True)
-    normed_ref[rows, :] = (floats * lax.rsqrt(mean + norm_epsilon) * gain_ref[...]).astype(jnp.bfloat16)
+    rows = pl.ds(pl.multiple_of(step * NORM_ROWS, NORM_ROWS), NORM_ROWS)
+    width = tok_ref.shape[1]
+    squares = jnp.zeros((NORM_ROWS, HD), jnp.float32)
+    for at in range(0, width, HD):
+        floats = tok_ref[rows, at:at + HD].astype(jnp.float32)
+        squares = squares + floats * floats
+    mean = jnp.sum(squares, axis=1, keepdims=True) * (1.0 / width)
+    factor = lax.rsqrt(mean + norm_epsilon)
+    for at in range(0, width, HD):
+        floats = tok_ref[rows, at:at + HD].astype(jnp.float32)
+        normed_ref[rows, at:at + HD] = (floats * factor * gain_ref[:, at:at + HD]).astype(jnp.bfloat16)
 
 
 def block_start(doc_ref, block):
@@ -64,14 +72,14 @@
     return raw * cos + pltpu.roll(raw, HD // 2, 1) * sin
 
 
-def project_kv(normed_ref, wkv_ref, cos_ref, sin_ref, kv_ref):
-    for half in range(2):
-        rows = pl.ds(half * 256, 256)
-        raw = jnp.dot(normed_ref[rows, :], wkv_ref[...], preferred_element_type=jnp.float32)
-        kv_ref[rows, :] = rotated(raw[:, :HD], cos_ref[rows, :], sin_ref[rows, :]).astype(jnp.bfloat16)
-        for b in range(2):
-            at = ROWS + (half * 2 + b) * BLK
-            kv_ref[at:at + BLK, :] = raw[b * BLK:(b + 1) * BLK, HD:].T.astype(jnp.bfloat16)
+def project_kv(normed_ref, wkv_ref, cos_ref, sin_ref, kv_ref, half):
+    rows = pl.ds(half * 256, 256)
+    raw = jnp.dot(normed_ref[rows, :], wkv_ref[...], preferred_element_type=jnp.float32)
+    keys = rotated(raw[:, :HD], cos_ref[rows, :], sin_ref[rows, :]).astype(jnp.bfloat16)
+    for b in range(2):
+        at = (half * 2 + b) * 2 * BLK
+        kv_ref[at:at + BLK, :] = keys[b * BLK:(b + 1) * BLK]
+        kv_ref[at + BLK:at + 2 * BLK, :] = raw[b * BLK:(b + 1) * BLK, HD:].T.astype(jnp.bfloat16)
 
 
 def project_q(normed_ref, wq_ref, cos_ref, sin_ref, q_ref, doc_ref, shard):
@@ -95,8 +103,9 @@
         jnp.where(lane == doc_ref[shard * BLOCKS + b], 0.0, FAR).astype(jnp.bfloat16)
         for b in range(BLOCKS)
     ]
-    keys = jnp.concatenate([kv_ref[slot, :ROWS, :], jnp.concatenate(marks, axis=0)], axis=1)
-    columns = [kv_ref[slot, ROWS + b * BLK:ROWS + (b + 1) * BLK, :] for b in range(BLOCKS)]
+    pieces = [kv_ref[slot, 2 * b * BLK:(2 * b + 1) * BLK, :] for b in range(BLOCKS)]
+    keys = jnp.concatenate([jnp.concatenate(pieces, axis=0), jnp.concatenate(marks, axis=0)], axis=1)
+    columns = [kv_ref[slot, (2 * b + 1) * BLK:(2 * b + 2) * BLK, :] for b in range(BLOCKS)]
     values = jnp.concatenate(
         [jnp.concatenate(columns, axis=1), jnp.ones((16, ROWS), jnp.bfloat16)], axis=0
     )
@@ -168,8 +177,8 @@
     loads.append(pltpu.make_async_copy(wv_hbm, wkv_ref.at[:, HD:], load_sem.at[5]))
     loads.append(pltpu.make_async_copy(wq_hbm, wq_ref, load_sem.at[6]))
     loads.append(pltpu.make_async_copy(wo_hbm, wo_ref, load_sem.at[7]))
-    for load in loads:
-        load.start()
+    for n in (0, 4, 5, 1, 2, 3):
+        loads[n].start()
 
     barrier = pltpu.get_barrier_semaphore()
     near = [at_seq(z, y + 1), at_seq(z, y - 1), at_seq(z + 1, y), at_seq(z - 1, y)]
@@ -188,16 +197,6 @@
         pl.semaphore_signal(barrier, inc=1, device_id=(3, part), device_id_type=MESH)
 
     make_tables(doc_ref, freq_ref, cos_ref, sin_ref, shard)
-    for n in range(4):
-        loads[n].wait()
-        lax.fori_loop(n * 8, n * 8 + 8, lambda i, s: (norm_rows(tok_ref, gain_ref, normed_ref, i), s)[1], 0)
-    loads[4].wait()
-    loads[5].wait()
-    own = y
-    project_kv(normed_ref, wkv_ref, cos_ref, sin_ref, kv_ref.at[own])
-
-    pl.semaphore_wait(barrier, len(near) + (first_corner | last_corner).astype(jnp.int32))
-
     def slot_of(j, step):
         return j * 4 + (y + step + 4) % 4
 
@@ -222,13 +221,16 @@
         transfers["pass left", j] = (j * 4 + 3, slot_of(j, 1), slot_of(j, 1), down)
     transfers["onward", 0] = (12, slot_of(0, 0), slot_of(1, 0), onward)
     transfers["onward", 1] = (13, slot_of(1, 0), slot_of(2, 0), onward)
-    transfers["corner", 0] = (14, slot_of(0, 0), 12, (12, part))
+    transfers["beside", 0] = (14, slot_of(0, -1), slot_of(1, -1), onward)
+    transfers["corner", 0] = (15, slot_of(0, 0), 12, (12, part))
     sends = {
         ("right", 0): y <= 2, ("left", 0): y == 0, ("pass right", 0): y == 2, ("pass left", 0): y == 3,
-        ("right", 1): z >= 1, ("left", 1): z >= 1, ("pass left", 1): z >= 1,
+        ("right", 1): (z >= 1) & (y == 3), ("left", 1): z >= 1,
+        ("pass right", 1): (z >= 1) & (y != 2), ("pass left", 1): (z >= 1) & (y == 0),
         ("right", 2): z >= 2, ("left", 2): (z >= 2) & (y >= 1),
-        ("pass right", 2): (z >= 2) & (y == 3), ("pass left", 2): (z >= 2) & (y == 2),
-        ("onward", 0): z <= 2, ("onward", 1): (z >= 1) & (z <= 2), ("corner", 0): first_corner,
+        ("pass left", 2): (z >= 2) & ((y == 1) | (y == 2)),
+        ("onward", 0): z <= 2, ("onward", 1): (z >= 1) & (z <= 2), ("beside", 0): (z <= 2) & (y >= 1),
+        ("corner", 0): first_corner,
     }
     arrives = {
         (0, -1): y >= 1, (0, 1): y == 3, (0, 2): y >= 2,
@@ -237,41 +239,61 @@
         (3, 0): last_corner,
     }
 
-    def start(*keys):
-        for key in keys:
-            @pl.when(sends[key])
-            def _(key=key):
-                for piece in range(PIECES):
-                    move(*transfers[key], piece).start()
-
-    def arrive(key, *then):
-        j, step = key
-        slot = 12 if j == 3 else slot_of(j, step)
-
-        @pl.when(arrives[key])
+    def start(key, piece):
+        @pl.when(sends[key])
         def _():
-            for piece in range(PIECES):
-                move(0, slot, slot, up, piece).wait_recv()
-                for other in then:
-                    @pl.when(sends[other])
-                    def _(other=other):
-                        move(*transfers[other], piece).start()
-
-    start(("onward", 0), ("right", 0), ("left", 0), ("corner", 0))
+            move(*transfers[key], piece).start()
+
+    def arrive(events):
+        for piece in range(PIECES):
+            for key, *then in events:
+                j, step = key
+                slot = 12 if j == 3 else slot_of(j, step)
+
+                @pl.when(arrives[key])
+                def _(slot=slot, then=then):
+                    move(0, slot, slot, up, piece).wait_recv()
+                    for other in then:
+                        start(other, piece)
+
+    own = y
+    per = BLK // NORM_ROWS
+    for piece in range(PIECES):
+        for n in (2 * piece, 2 * piece + 1):
+            loads[n].wait()
+            if n == 3:
+                loads[6].start()
+                loads[7].start()
+            lax.fori_loop(
+                n * per, n * per + per, lambda i, s: (norm_rows(tok_ref, gain_ref, normed_ref, i), s)[1], 0
+            )
+        if piece == 0:
+            loads[4].wait()
+            loads[5].wait()
+        project_kv(normed_ref, wkv_ref, cos_ref, sin_ref, kv_ref.at[own], piece)
+        if piece == 0:
+            pl.semaphore_wait(barrier, len(near) + (first_corner | last_corner).astype(jnp.int32))
+        for key in (("onward", 0), ("right", 0), ("left", 0), ("corner", 0)):
+            start(key, piece)
+
     loads[6].wait()
     project_q(normed_ref, wq_ref, cos_ref, sin_ref, q_ref, doc_ref, shard)
     fold_own(q_ref, *slot_pair(kv_ref, own, doc_ref, shard), m_ref, acc_ref)
 
     order = [
-        ((0, -1), [((1, 0), ("onward", 1), ("right", 1), ("left", 1)), ((0, -1), ("pass right", 0))]),
-        ((1, 0), [((0, 1), ("pass left", 0))]),
+        ((0, -1), [
+            ((1, 0), ("onward", 1), ("left", 1), ("right", 1)),
+            ((0, -1), ("pass right", 0), ("beside", 0)),
+            ((0, 1), ("pass left", 0)),
+        ]),
+        ((1, 0), []),
         ((0, 1), []),
-        ((1, 1), [((2, 0), ("right", 2), ("left", 2)), ((1, 1), ("pass left", 1))]),
+        ((1, 1), [((2, 0), ("left", 2), ("right", 2)), ((1, 1), ("pass left", 1))]),
         ((0, 2), [((0, 2),)]),
-        ((1, -1), [((1, -1),)]),
-        ((2, 0), [((2, -1), ("pass right", 2)), ((2, 1), ("pass left", 2))]),
-        ((2, -1), []),
+        ((2, 0), []),
+        ((1, -1), [((2, 1), ("pass left", 2)), ((1, -1), ("pass right", 1))]),
         ((2, 1), []),
+        ((2, -1), [((2, -1),)]),
         ((1, 2), [((1, 2),)]),
         ((2, 2), [((2, 2),)]),
         ((3, 0), [((3, 0),)]),
@@ -283,8 +305,7 @@
             if events:
                 @pl.when(k == n)
                 def _(events=events):
-                    for event in events:
-                        arrive(*event)
+                    arrive(events)
             here = k == n
             row = jnp.where(here, key[0], row)
             turn = jnp.where(here, (y + key[1] + 4) % 4, turn)
@@ -309,69 +330,90 @@
     loads[7].wait()
     half = wo_ref.shape[1] // 2
 
-    def give(k):
+    def give(k, h):
         return pltpu.make_async_remote_copy(
-            src_ref=give_ref.at[k], dst_ref=take_ref.at[k], send_sem=give_send.at[k], recv_sem=give_recv.at[k],
+            src_ref=give_ref.at[k, h], dst_ref=take_ref.at[k, h],
+            send_sem=give_send.at[2 * k + h], recv_sem=give_recv.at[2 * k + h],
             device_id=at_tp(x, 1 - c), device_id_type=MESH,
         )
 
-    def halves(h):
+    def first(h):
         return pltpu.make_async_remote_copy(
             src_ref=pass_ref.at[0, h], dst_ref=half_ref.at[h], send_sem=pass_send.at[h], recv_sem=half_recv.at[h],
             device_id=at_tp(x + 1 - 2 * h, c), device_id_type=MESH,
         )
 
-    def lasts(k):
+    def final(k, h):
         return pltpu.make_async_remote_copy(
-            src_ref=pass_ref.at[k], dst_ref=last_ref.at[k - 1], send_sem=pass_send.at[1 + k], recv_sem=last_recv.at[k - 1],
+            src_ref=pass_ref.at[k, h], dst_ref=last_ref.at[k - 1, h],
+            send_sem=pass_send.at[2 * k + h], recv_sem=last_recv.at[2 * k - 2 + h],
             device_id=at_tp(x + 3 - 2 * k, c), device_id_type=MESH,
         )
 
-    def project(k, carry):
-        i = jnp.where(k == 0, x + 2, jnp.where(k == 1, x + 1, jnp.where(k == 2, x + 3, x))) % 4
-        write_context(acc_ref, i, ctx_ref)
-        theirs = ctx_ref[pl.ds(pl.multiple_of((1 - c) * 64, 64), 64), :]
-        ours = ctx_ref[pl.ds(pl.multiple_of(c * 64, 64), 64), :]
+    targets = [(x + 2) % 4, (x + 1) % 4, (x + 3) % 4, x]
+
+    def context(k):
+        write_context(acc_ref, targets[k], ctx_ref.at[k])
+
+    def project(k, h):
+        theirs = ctx_ref[k, pl.ds(pl.multiple_of((1 - c) * 64, 64), 64), :]
+        ours = ctx_ref[k, pl.ds(pl.multiple_of(c * 64, 64), 64), :]
         both = jnp.concatenate([theirs, ours], axis=0)
-        product = jnp.dot(both, wo_ref[...], preferred_element_type=jnp.float32)
-        for h in range(2):
-            columns = slice(h * half, (h + 1) * half)
-            give_ref[k, h] = product[:64, columns].astype(jnp.bfloat16)
-            mine_ref[k, h] = product[64:, columns]
-        give(k).start()
-        return carry
+        product = jnp.dot(both, wo_ref[:, h * half:(h + 1) * half], preferred_element_type=jnp.float32)
+        give_ref[k, h] = product[:64].astype(jnp.bfloat16)
+        give(k, h).start()
+        mine_ref[k, h] = product[64:]
 
     def paired(k, h):
+        give(k, h).wait_recv()
         return mine_ref[k, h] + take_ref[k, h].astype(jnp.float32)
 
-    lax.fori_loop(0, 2, project, 0)
-    give(0).wait_recv()
+    def send_first(h):
+        pass_ref[0, h] = paired(0, h).astype(jnp.bfloat16)
+        first(h).start()
+
+    def send_final(k, h, forward):
+        total = paired(k, h)
+        if forward:
+            first(h).wait_recv()
+            total = total + half_ref[h].astype(jnp.float32)
+        pass_ref[k, h] = total.astype(jnp.bfloat16)
+        final(k, h).start()
+
+    context(0)
+    project(0, 0)
+    project(0, 1)
+    context(1)
+    send_first(0)
+    project(1, 1)
+    send_first(1)
+    context(2)
+    project(2, 0)
+    send_final(1, 1, False)
+    project(1, 0)
+    send_final(2, 0, False)
+    project(2, 1)
+    context(3)
+    project(3, 0)
+    project(3, 1)
+    send_final(1, 0, True)
+    send_final(2, 1, True)
     for h in range(2):
-        pass_ref[0, h] = paired(0, h).astype(jnp.bfloat16)
-        halves(h).start()
-    lax.fori_loop(2, 4, project, 0)
-    for k in (1, 2):
-        give(k).wait_recv()
-        halves(k - 1).wait_recv()
-        for h in range(2):
-            total = paired(k, h)
-            if h == k - 1:
-                total = total + half_ref[h].astype(jnp.float32)
-            pass_ref[k, h] = total.astype(jnp.bfloat16)
-        lasts(k).start()
-    give(3).wait_recv()
+        early = 2 - h
+        total = paired(3, h)
+        final(early, h).wait_recv()
+        mine_ref[3, h] = total + last_ref[early - 1, h].astype(jnp.float32)
     for h in range(2):
-        mine_ref[3, h] = paired(3, h)
-    lasts(1).wait_recv()
-    lasts(2).wait_recv()
+        late = 1 + h
+        final(late, h).wait_recv()
+        total = mine_ref[3, h] + last_ref[late - 1, h].astype(jnp.float32)
+        out_ref[:, h * half:(h + 1) * half] = total.astype(jnp.bfloat16)
     for h in range(2):
-        total = mine_ref[3, h] + last_ref[0, h].astype(jnp.float32) + last_ref[1, h].astype(jnp.float32)
-        out_ref[:, h * half:(h + 1) * half] = total.astype(jnp.bfloat16)
-    for k in range(4):
-        give(k).wait_send()
-    for h in range(2):
-        halves(h).wait_send()
-        lasts(h + 1).wait_send()
+        for k in range(4):
+            give(k, h).wait_send()
+        first(h).wait_send()
+        final(1, h).wait_send()
+        final(2, h).wait_send()
 
 
 def local(tokens, norm_gain, w_query, w_key, w_value, w_out, doc_ids):
@@ -399,14 +441,14 @@
             pltpu.VMEM((13, 2 * ROWS, HD), b16),
             pltpu.VMEM((BLOCKS, 8, HEADS * BLK), f32),
             pltpu.VMEM((BLOCKS, HD + 16, HEADS * BLK), f32),
-            pltpu.VMEM((BLK, HEADS * HD), b16),
+            pltpu.VMEM((4, BLK, HEADS * HD), b16),
             pltpu.VMEM((4, 2, 64, half), f32),
             pltpu.VMEM((4, 2, 64, half), b16),
             pltpu.VMEM((4, 2, 64, half), b16),
             pltpu.VMEM((3, 2, 64, half), b16),
             pltpu.VMEM((2, 64, half), b16),
             pltpu.VMEM((2, 2, 64, half), b16),
-            dma((8,)), dma((15 * PIECES,)), dma((13 * PIECES,)), dma((4,)), dma((4,)), dma((4,)), dma((2,)), dma((2,)),
+            dma((8,)), dma((16 * PIECES,)), dma((13 * PIECES,)), dma((8,)), dma((8,)), dma((6,)), dma((2,)), dma((4,)),
         ],
         compiler_params=pltpu.CompilerParams(
             vmem_limit_bytes=58 * 2**20, collective_id=0, has_side_effects=True

time: 71.3 us -> 66.8 us (0.937)
  Pallas kernels: 69.2 us -> 64.4 us
    pallas_call x1, Pallas kernels: 69.2 us -> 64.4 us  [local(): pl.pallas_call(kernel, out_shape=jax.ShapeDtypeStruct((64, w_out.shape[1]...]
where the time goes in v3:
time: 66.8 us; the launch traced here: 66.3 us
  Pallas kernels  64.4 us (96%)
  local copies, waits for them, and re-layouts  1.87 us (3%)
    pallas_call x1, Pallas kernels, local(): pl.pallas_call(kernel, out_shape=jax.ShapeDtypeStruct((64, w_out.shape[1]...  64.4 us
    unnamed x1, local copies, waits for them, and re-layouts  1.87 us

profile of v3, /device:TPU:96, one launch (start us, length us, event | category | flops | bytes accessed | tf_op | source)
XLA Modules:
  0.0 66.3 jit_solution(2441788013345090926)
XLA Ops:
  0.0 64.4 %shard_map.82 = bf16[64,4096]{1,0:T(8,128)(2,1)} custom-call(s32[64]{0:T(128)} %doc_ref.1, bf16[512,4096]{1,0:T(8,128)(2,1)} %tok_hbm.1, f32[1,4096]{1,0:T(1,128)} %bitcast.1, bf16[4096,512]{1,0:T(8,128)(2,1)} %wq_hbm.1, bf16[4096,128]{1,0:T(8,128)(2,1)} %wk_hbm.1, bf16[4096,128]{1,0:T(8,128)(2,1)} %wv_hbm.1, f32[1,128]{1,0:T(1,128)} %constant.2.clone.freq_ref, ...), custom_call_target="tpu_custom_call" | custom-call | flops 10000000000 | bytes 15728640 | tf_op jit(solution)/shard_map/pallas_call | solution.py:427
  64.5 1.9 %copy.10 = bf16[64,4096]{1,0:T(8,128)(2,1)} copy(bf16[64,4096]{1,0:T(8,128)(2,1)} %shard_map.82) | data formatting | bytes 1048576

commit v4 on v3

--- a/solution.py
+++ b/solution.py
@@ -14,6 +14,7 @@
 BLOCKS = ROWS // BLK
 HEADS = 4
 PIECES = 2
+CUTS = 8
 NORM_ROWS = 32
 MESH = pl.DeviceIdType.MESH
 FAR = -1e30
@@ -155,7 +156,7 @@
 def kernel(
     doc_ref, tok_hbm, gain_ref, wq_hbm, wk_hbm, wv_hbm, freq_ref, wo_hbm, out_ref,
     tok_ref, wkv_ref, wq_ref, wo_ref, normed_ref, cos_ref, sin_ref, q_ref, kv_ref, m_ref, acc_ref,
-    ctx_ref, mine_ref, give_ref, take_ref, pass_ref, half_ref, last_ref,
+    ctx_ref, rows_ref, mine_ref, give_ref, take_ref, pass_ref, half_ref, last_ref,
     load_sem, kv_send, kv_recv, give_send, give_recv, pass_send, half_recv, last_recv,
 ):
     shard = lax.axis_index("seq")
@@ -235,6 +236,7 @@
     arrives = {
         (0, -1): y >= 1, (0, 1): y == 3, (0, 2): y >= 2,
         (1, 0): z >= 1, (1, -1): z >= 1, (1, 1): z >= 1, (1, 2): z >= 1,
+        (1, -1, 0): (z >= 1) & (y == 0), (1, -1, 1): (z >= 1) & (y >= 1),
         (2, 0): z >= 2, (2, -1): z >= 2, (2, 1): (z >= 2) & (y <= 2), (2, 2): (z >= 2) & (y <= 1),
         (3, 0): last_corner,
     }
@@ -247,7 +249,7 @@
     def arrive(events):
         for piece in range(PIECES):
             for key, *then in events:
-                j, step = key
+                j, step = key[:2]
                 slot = 12 if j == 3 else slot_of(j, step)
 
                 @pl.when(arrives[key])
@@ -287,16 +289,20 @@
             ((0, 1), ("pass left", 0)),
         ]),
         ((1, 0), []),
-        ((0, 1), []),
-        ((1, 1), [((2, 0), ("left", 2), ("right", 2)), ((1, 1), ("pass left", 1))]),
+        ((0, 1), [((3, 0),)]),
+        ((3, 0), []),
+        ((1, 1), [
+            ((2, 0), ("left", 2), ("right", 2)),
+            ((1, 1), ("pass left", 1)),
+            ((1, -1, 0), ("pass right", 1)),
+        ]),
         ((0, 2), [((0, 2),)]),
         ((2, 0), []),
-        ((1, -1), [((2, 1), ("pass left", 2)), ((1, -1), ("pass right", 1))]),
+        ((1, -1), [((2, 1), ("pass left", 2)), ((1, -1, 1), ("pass right", 1))]),
         ((2, 1), []),
         ((2, -1), [((2, -1),)]),
         ((1, 2), [((1, 2),)]),
         ((2, 2), [((2, 2),)]),
-        ((3, 0), [((3, 0),)]),
     ]
 
     def step(k, carry):
@@ -328,92 +334,87 @@
                 move(*transfers[key], piece).wait_send()
 
     loads[7].wait()
-    half = wo_ref.shape[1] // 2
-
-    def give(k, h):
+    span = wo_ref.shape[1] // CUTS
+
+    def give(n):
         return pltpu.make_async_remote_copy(
-            src_ref=give_ref.at[k, h], dst_ref=take_ref.at[k, h],
-            send_sem=give_send.at[2 * k + h], recv_sem=give_recv.at[2 * k + h],
+            src_ref=give_ref.at[n], dst_ref=take_ref.at[n], send_sem=give_send.at[n], recv_sem=give_recv.at[n],
             device_id=at_tp(x, 1 - c), device_id_type=MESH,
         )
 
-    def first(h):
+    def first(n):
         return pltpu.make_async_remote_copy(
-            src_ref=pass_ref.at[0, h], dst_ref=half_ref.at[h], send_sem=pass_send.at[h], recv_sem=half_recv.at[h],
-            device_id=at_tp(x + 1 - 2 * h, c), device_id_type=MESH,
+            src_ref=pass_ref.at[0, n], dst_ref=half_ref.at[n], send_sem=pass_send.at[n], recv_sem=half_recv.at[n],
+            device_id=at_tp(x + (1 if n < CUTS // 2 else -1), c), device_id_type=MESH,
         )
 
-    def final(k, h):
+    def final(k, n):
         return pltpu.make_async_remote_copy(
-            src_ref=pass_ref.at[k, h], dst_ref=last_ref.at[k - 1, h],
-            send_sem=pass_send.at[2 * k + h], recv_sem=last_recv.at[2 * k - 2 + h],
+            src_ref=pass_ref.at[k, n], dst_ref=last_ref.at[k - 1, n],
+            send_sem=pass_send.at[CUTS * k + n], recv_sem=last_recv.at[CUTS * (k - 1) + n],
             device_id=at_tp(x + 3 - 2 * k, c), device_id_type=MESH,
         )
 
     targets = [(x + 2) % 4, (x + 1) % 4, (x + 3) % 4, x]
-
-    def context(k):
+    for k in range(4):
         write_context(acc_ref, targets[k], ctx_ref.at[k])
-
-    def project(k, h):
-        theirs = ctx_ref[k, pl.ds(pl.multiple_of((1 - c) * 64, 64), 64), :]
-        ours = ctx_ref[k, pl.ds(pl.multiple_of(c * 64, 64), 64), :]
-        both = jnp.concatenate([theirs, ours], axis=0)
-        product = jnp.dot(both, wo_ref[:, h * half:(h + 1) * half], preferred_element_type=jnp.float32)
-        give_ref[k, h] = product[:64].astype(jnp.bfloat16)
-        give(k, h).start()
-        mine_ref[k, h] = product[64:]
-
-    def paired(k, h):
-        give(k, h).wait_recv()
-        return mine_ref[k, h] + take_ref[k, h].astype(jnp.float32)
-
-    def send_first(h):
-        pass_ref[0, h] = paired(0, h).astype(jnp.bfloat16)
-        first(h).start()
-
-    def send_final(k, h, forward):
-        total = paired(k, h)
-        if forward:
-            first(h).wait_recv()
-            total = total + half_ref[h].astype(jnp.float32)
-        pass_ref[k, h] = total.astype(jnp.bfloat16)
-        final(k, h).start()
-
-    context(0)
-    project(0, 0)
-    project(0, 1)
-    context(1)
-    send_first(0)
-    project(1, 1)
-    send_first(1)
-    context(2)
-    project(2, 0)
-    send_final(1, 1, False)
-    project(1, 0)
-    send_final(2, 0, False)
-    project(2, 1)
-    context(3)
-    project(3, 0)
-    project(3, 1)
-    send_final(1, 0, True)
-    send_final(2, 1, True)
-    for h in range(2):
-        early = 2 - h
-        total = paired(3, h)
-        final(early, h).wait_recv()
-        mine_ref[3, h] = total + last_ref[early - 1, h].astype(jnp.float32)
-    for h in range(2):
-        late = 1 + h
-        final(late, h).wait_recv()
-        total = mine_ref[3, h] + last_ref[late - 1, h].astype(jnp.float32)
-        out_ref[:, h * half:(h + 1) * half] = total.astype(jnp.bfloat16)
-    for h in range(2):
+    theirs = pl.ds(pl.multiple_of((1 - c) * 64, 64), 64)
+    ours = pl.ds(pl.multiple_of(c * 64, 64), 64)
+    for k in range(4):
+        rows_ref[k * 64:(k + 1) * 64, :] = ctx_ref[k, theirs, :]
+        rows_ref[(4 + k) * 64:(5 + k) * 64, :] = ctx_ref[k, ours, :]
+
+    def project(n):
+        product = jnp.dot(
+            rows_ref[...], wo_ref[:, n * span:(n + 1) * span], preferred_element_type=jnp.float32
+        )
         for k in range(4):
-            give(k, h).wait_send()
-        first(h).wait_send()
-        final(1, h).wait_send()
-        final(2, h).wait_send()
+            give_ref[n, k] = product[k * 64:(k + 1) * 64].astype(jnp.bfloat16)
+        give(n).start()
+        for k in range(4):
+            mine_ref[n, k] = product[(4 + k) * 64:(5 + k) * 64]
+
+    def paired(k, n):
+        return mine_ref[n, k] + take_ref[n, k].astype(jnp.float32)
+
+    def send_early(n):
+        give(n).wait_recv()
+        pass_ref[0, n] = paired(0, n).astype(jnp.bfloat16)
+        first(n).start()
+        k = 2 if n < CUTS // 2 else 1
+        pass_ref[k, n] = paired(k, n).astype(jnp.bfloat16)
+        final(k, n).start()
+
+    def send_late(n):
+        k = 1 if n < CUTS // 2 else 2
+        total = paired(k, n)
+        first(n).wait_recv()
+        pass_ref[k, n] = (total + half_ref[n].astype(jnp.float32)).astype(jnp.bfloat16)
+        final(k, n).start()
+
+    turn = [n // 2 + (n % 2) * (CUTS // 2) for n in range(CUTS)]
+    for at in range(CUTS + 1):
+        if at < CUTS:
+            project(turn[at])
+        if at > 0:
+            send_early(turn[at - 1])
+    for n in turn:
+        send_late(n)
+    for n in turn:
+        k = 2 if n < CUTS // 2 else 1
+        total = paired(3, n)
+        final(k, n).wait_recv()
+        mine_ref[n, 3] = total + last_ref[k - 1, n].astype(jnp.float32)
+    for n in turn:
+        k = 1 if n < CUTS // 2 else 2
+        final(k, n).wait_recv()
+        total = mine_ref[n, 3] + last_ref[k - 1, n].astype(jnp.float32)
+        out_ref[:, n * span:(n + 1) * span] = total.astype(jnp.bfloat16)
+    for n in range(CUTS):
+        give(n).wait_send()
+        first(n).wait_send()
+        final(1, n).wait_send()
+        final(2, n).wait_send()
 
 
 def local(tokens, norm_gain, w_query, w_key, w_value, w_out, doc_ids):
@@ -421,7 +422,7 @@
     smem = pl.BlockSpec(memory_space=pltpu.SMEM)
     hbm = pl.BlockSpec(memory_space=pl.ANY)
     width = tokens.shape[1]
-    half = w_out.shape[1] // 2
+    span = w_out.shape[1] // CUTS
     b16, f32 = jnp.bfloat16, jnp.float32
     dma = pltpu.SemaphoreType.DMA
     return pl.pallas_call(
@@ -442,13 +443,15 @@
             pltpu.VMEM((BLOCKS, 8, HEADS * BLK), f32),
             pltpu.VMEM((BLOCKS, HD + 16, HEADS * BLK), f32),
             pltpu.VMEM((4, BLK, HEADS * HD), b16),
-            pltpu.VMEM((4, 2, 64, half), f32),
-            pltpu.VMEM((4, 2, 64, half), b16),
-            pltpu.VMEM((4, 2, 64, half), b16),
-            pltpu.VMEM((3, 2, 64, half), b16),
-            pltpu.VMEM((2, 64, half), b16),
-            pltpu.VMEM((2, 2, 64, half), b16),
-            dma((8,)), dma((16 * PIECES,)), dma((13 * PIECES,)), dma((8,)), dma((8,)), dma((6,)), dma((2,)), dma((4,)),
+            pltpu.VMEM((8 * 64, HEADS * HD), b16),
+            pltpu.VMEM((CUTS, 4, 64, span), f32),
+            pltpu.VMEM((CUTS, 4, 64, span), b16),
+            pltpu.VMEM((CUTS, 4, 64, span), b16),
+            pltpu.VMEM((3, CUTS, 64, span), b16),
+            pltpu.VMEM((CUTS, 64, span), b16),
+            pltpu.VMEM((2, CUTS, 64, span), b16),
+            dma((8,)), dma((16 * PIECES,)), dma((13 * PIECES,)),
+            dma((CUTS,)), dma((CUTS,)), dma((3 * CUTS,)), dma((CUTS,)), dma((2 * CUTS,)),
         ],
         compiler_params=pltpu.CompilerParams(
             vmem_limit_bytes=58 * 2**20, collective_id=0, has_side_effects=True

time: 66.8 us -> 65.3 us (0.978)
  Pallas kernels: 64.4 us -> 62.9 us
    pallas_call x1, Pallas kernels: 64.4 us -> 62.9 us  [local(): pl.pallas_call(kernel, out_shape=jax.ShapeDtypeStruct((64, w_out.shape[1]...]
where the time goes in v4:
time: 65.3 us; the launch traced here: 64.8 us
  Pallas kernels  62.9 us (96%)
  local copies, waits for them, and re-layouts  1.87 us (3%)
    pallas_call x1, Pallas kernels, local(): pl.pallas_call(kernel, out_shape=jax.ShapeDtypeStruct((64, w_out.shape[1]...  62.9 us
    unnamed x1, local copies, waits for them, and re-layouts  1.87 us

profile of v4, /device:TPU:96, one launch (start us, length us, event | category | flops | bytes accessed | tf_op | source)
XLA Modules:
  0.0 64.8 jit_solution(17015202556856906444)
XLA Ops:
  0.0 62.9 %shard_map.82 = bf16[64,4096]{1,0:T(8,128)(2,1)} custom-call(s32[64]{0:T(128)} %doc_ref.1, bf16[512,4096]{1,0:T(8,128)(2,1)} %tok_hbm.1, f32[1,4096]{1,0:T(1,128)} %bitcast.1, bf16[4096,512]{1,0:T(8,128)(2,1)} %wq_hbm.1, bf16[4096,128]{1,0:T(8,128)(2,1)} %wk_hbm.1, bf16[4096,128]{1,0:T(8,128)(2,1)} %wv_hbm.1, f32[1,128]{1,0:T(1,128)} %constant.2.clone.freq_ref, ...), custom_call_target="tpu_custom_call" | custom-call | flops 10000000000 | bytes 15728640 | tf_op jit(solution)/shard_map/pallas_call | solution.py:428
  62.9 1.9 %copy.10 = bf16[64,4096]{1,0:T(8,128)(2,1)} copy(bf16[64,4096]{1,0:T(8,128)(2,1)} %shard_map.82) | data formatting | bytes 1048576

commit v5 on v4

--- a/solution.py
+++ b/solution.py
@@ -223,6 +223,7 @@
     transfers["onward", 0] = (12, slot_of(0, 0), slot_of(1, 0), onward)
     transfers["onward", 1] = (13, slot_of(1, 0), slot_of(2, 0), onward)
     transfers["beside", 0] = (14, slot_of(0, -1), slot_of(1, -1), onward)
+    transfers["later", 0] = transfers["beside", 0]
     transfers["corner", 0] = (15, slot_of(0, 0), 12, (12, part))
     sends = {
         ("right", 0): y <= 2, ("left", 0): y == 0, ("pass right", 0): y == 2, ("pass left", 0): y == 3,
@@ -230,7 +231,8 @@
         ("pass right", 1): (z >= 1) & (y != 2), ("pass left", 1): (z >= 1) & (y == 0),
         ("right", 2): z >= 2, ("left", 2): (z >= 2) & (y >= 1),
         ("pass left", 2): (z >= 2) & ((y == 1) | (y == 2)),
-        ("onward", 0): z <= 2, ("onward", 1): (z >= 1) & (z <= 2), ("beside", 0): (z <= 2) & (y >= 1),
+        ("onward", 0): z <= 2, ("onward", 1): (z >= 1) & (z <= 2), ("beside", 0): (z == 0) & (y >= 1),
+        ("later", 0): (z >= 1) & (z <= 2) & (y >= 1),
         ("corner", 0): first_corner,
     }
     arrives = {
@@ -263,8 +265,9 @@
     for piece in range(PIECES):
         for n in (2 * piece, 2 * piece + 1):
             loads[n].wait()
+            if n == 2:
+                loads[6].start()
             if n == 3:
-                loads[6].start()
                 loads[7].start()
             lax.fori_loop(
                 n * per, n * per + per, lambda i, s: (norm_rows(tok_ref, gain_ref, normed_ref, i), s)[1], 0
@@ -310,8 +313,11 @@
         for n, (key, events) in enumerate(order):
             if events:
                 @pl.when(k == n)
-                def _(events=events):
+                def _(events=events, n=n):
                     arrive(events)
+                    if n == 2:
+                        for piece in range(PIECES):
+                            start(("later", 0), piece)
             here = k == n
             row = jnp.where(here, key[0], row)
             turn = jnp.where(here, (y + key[1] + 4) % 4, turn)
@@ -327,12 +333,6 @@
         return carry
 
     lax.fori_loop(0, len(order), step, 0)
-    for key in sends:
-        @pl.when(sends[key])
-        def _(key=key):
-            for piece in range(PIECES):
-                move(*transfers[key], piece).wait_send()
-
     loads[7].wait()
     span = wo_ref.shape[1] // CUTS
 
@@ -410,6 +410,12 @@
         final(k, n).wait_recv()
         total = mine_ref[n, 3] + last_ref[k - 1, n].astype(jnp.float32)
         out_ref[:, n * span:(n + 1) * span] = total.astype(jnp.bfloat16)
+    for key in sends:
+        @pl.when(sends[key])
+        def _(key=key):
+            for piece in range(PIECES):
+                move(*transfers[key], piece).wait_send()
+
     for n in range(CUTS):
         give(n).wait_send()
         first(n).wait_send()

time: 65.3 us -> 64.5 us (0.988)
  the two profiles are of different devices: /device:TPU:96 before, /device:TPU:105 now
where the time goes in v5:
time: 64.5 us; the launch traced here: 64.3 us
  Pallas kernels  62.5 us (97%)
  local copies, waits for them, and re-layouts  1.87 us (3%)
    pallas_call x1, Pallas kernels, local(): pl.pallas_call(kernel, out_shape=jax.ShapeDtypeStruct((64, w_out.shape[1]...  62.5 us
    unnamed x1, local copies, waits for them, and re-layouts  1.87 us

profile of v5, /device:TPU:105, one launch (start us, length us, event | category | flops | bytes accessed | tf_op | source)
XLA Modules:
  0.0 64.3 jit_solution(15909092196380697095)
XLA Ops:
  0.0 62.5 %shard_map.82 = bf16[64,4096]{1,0:T(8,128)(2,1)} custom-call(s32[64]{0:T(128)} %doc_ref.1, bf16[512,4096]{1,0:T(8,128)(2,1)} %tok_hbm.1, f32[1,4096]{1,0:T(1,128)} %bitcast.1, bf16[4096,512]{1,0:T(8,128)(2,1)} %wq_hbm.1, bf16[4096,128]{1,0:T(8,128)(2,1)} %wk_hbm.1, bf16[4096,128]{1,0:T(8,128)(2,1)} %wv_hbm.1, f32[1,128]{1,0:T(1,128)} %constant.2.clone.freq_ref, ...), custom_call_target="tpu_custom_call" | custom-call | flops 10000000000 | bytes 15728640 | tf_op jit(solution)/shard_map/pallas_call | solution.py:434
  62.5 1.9 %copy.10 = bf16[64,4096]{1,0:T(8,128)(2,1)} copy(bf16[64,4096]{1,0:T(8,128)(2,1)} %shard_map.82) | data formatting | bytes 1048576
